TPU v7x, 256 devices: a whole 4x4x8 slice. The times are simulated.
256 devices in a mesh: wide: 32 (over x, z), narrow: 8 (over y, core).
Axes of the slice: x: 4, y: 4, z: 8, core: 2. Of those that a mesh axis runs over, the one named last changes fastest.
Arguments:
- latent: bfloat16 [8192, 4096], P('wide', 'narrow'), may hold values from -90 to 90
- actions: int32 [8192], P('wide'), may hold values from 0 to 255
- action_table: bfloat16 [256, 4096], P(None, 'narrow'), may hold values from -3 to 3
- norm1_gain: float32 [4096], P('narrow'), may hold values from 0.5 to 1.5
- w_query: bfloat16 [4096, 2048], P(None, 'narrow'), may hold values from -0.140625 to 0.140625
- w_key: bfloat16 [4096, 2048], P(None, 'narrow'), may hold values from -0.140625 to 0.140625
- w_value: bfloat16 [4096, 2048], P(None, 'narrow'), may hold values from -0.09375 to 0.09375
- w_out: bfloat16 [2048, 4096], P(None, 'narrow'), may hold values from -0.125 to 0.125
- key_cache: bfloat16 [64, 512, 2048], P('wide', None, 'narrow'), may hold values from -460 to 460
- value_cache: bfloat16 [64, 512, 2048], P('wide', None, 'narrow'), may hold values from -6 to 6
- norm2_gain: float32 [4096], P('narrow'), may hold values from 0.5 to 1.5
- policy_in: bfloat16 [4096, 512], P('narrow'), may hold values from -0.09375 to 0.09375
- value_in: bfloat16 [4096, 512], P('narrow'), may hold values from -0.09375 to 0.09375
- policy_out: bfloat16 [512, 256], replicated, may hold values from -12.5 to 12.5
- value_out: bfloat16 [512], replicated, may hold values from -0.25 to 0.25
- targets: int32 [8192], P('wide'), may hold values from 0 to 255
- returns: float32 [8192], P('wide'), may hold values from -19 to 19
Outputs:
- new_latent: bfloat16 [8192, 4096], P('wide', 'narrow')
- losses: float32 [2], replicated
- policy_in_grad: bfloat16 [4096, 512], P('narrow')
- value_in_grad: bfloat16 [4096, 512], P('narrow')
- policy_out_grad: bfloat16 [512, 256], replicated
- value_out_grad: bfloat16 [512], replicated
All inputs are finite; a program needn't handle non-finite values.
Results may differ from a plain program's by a relative error of at most 0.019.
Values may be sent and summed in bfloat16 or wider, within the bound.
A program may use at most 64 MiB of HBM per device.

v0:
```python
import jax
import jax.numpy as jnp
from jax import lax
from jax.sharding import PartitionSpec as P

HD = 128


EPSILON = 1e-05


def silu_slope(values):
    sigma = jax.nn.sigmoid(values)
    return sigma * (1.0 + values * (1.0 - sigma))


def per_device(
    latent,
    actions,
    action_table,
    norm1_gain,
    w_query,
    w_key,
    w_value,
    w_out,
    key_cache,
    value_cache,
    norm2_gain,
    policy_in,
    value_in,
    policy_out,
    value_out,
    targets,
    returns,
):
    row_count = latent.shape[0]
    scene_count = key_cache.shape[0]
    branch_count = row_count // scene_count
    width_local = latent.shape[1]
    full_width = width_local * lax.axis_size("narrow")
    heads_local = w_query.shape[1] // HD
    total_rows = row_count * lax.axis_size("wide")
    action_count = action_table.shape[0]
    action_onehot = (actions[:, None] == jnp.arange(action_count, dtype=jnp.int32)[None, :]).astype(
        jnp.bfloat16
    )
    tokens = latent.astype(jnp.float32) + jnp.dot(
        action_onehot, action_table, preferred_element_type=jnp.float32
    )
    squares = lax.psum(jnp.sum(tokens * tokens, axis=1), "narrow")
    inverse = lax.rsqrt(squares / full_width + EPSILON)
    normed = (tokens * inverse[:, None] * norm1_gain).astype(jnp.bfloat16)
    segment = lax.all_gather(normed, "narrow", axis=1, tiled=True)
    query, key_new, value_new = tuple(
        (
            jnp.dot(segment, matrix, preferred_element_type=jnp.float32)
            for matrix in (w_query, w_key, w_value)
        )
    )
    query = query.astype(jnp.bfloat16).reshape(scene_count, branch_count, heads_local, HD)
    key_new = key_new.astype(jnp.bfloat16).reshape(scene_count, branch_count, heads_local, HD)
    value_new = value_new.astype(jnp.bfloat16).reshape(scene_count, branch_count, heads_local, HD)
    cache_keys = key_cache.reshape(scene_count, key_cache.shape[1], heads_local, HD)
    cache_values = value_cache.reshape(scene_count, value_cache.shape[1], heads_local, HD)
    scaling = HD ** (-0.5)
    scores = (
        jnp.einsum("sbhd,schd->sbhc", query, cache_keys, preferred_element_type=jnp.float32)
        * scaling
    )
    own_score = jnp.sum(query.astype(jnp.float32) * key_new.astype(jnp.float32), axis=-1) * scaling
    highest = jnp.maximum(jnp.max(scores, axis=-1), own_score)
    expd = jnp.exp(scores - highest[..., None])
    own_exp = jnp.exp(own_score - highest)
    totals = jnp.sum(expd, axis=-1) + own_exp
    weights = (expd / totals[..., None]).astype(jnp.bfloat16)
    own_weight = (own_exp / totals).astype(jnp.bfloat16)
    mixed = jnp.einsum("sbhc,schd->sbhd", weights, cache_values, preferred_element_type=jnp.float32)
    mixed = mixed + own_weight.astype(jnp.float32)[..., None] * value_new.astype(jnp.float32)
    attended = mixed.astype(jnp.bfloat16).reshape(row_count, heads_local * HD)
    update = jnp.dot(
        lax.all_gather(attended, "narrow", axis=1, tiled=True),
        w_out,
        preferred_element_type=jnp.float32,
    )
    state = tokens + update
    new_latent = state.astype(jnp.bfloat16)
    squares_two = lax.psum(jnp.sum(state * state, axis=1), "narrow")
    inverse_two = lax.rsqrt(squares_two / full_width + EPSILON)
    heads_in = (state * inverse_two[:, None] * norm2_gain).astype(jnp.bfloat16)
    policy_pre, value_pre = lax.psum(
        (
            jnp.dot(heads_in, policy_in, preferred_element_type=jnp.float32),
            jnp.dot(heads_in, value_in, preferred_element_type=jnp.float32),
        ),
        "narrow",
    )
    policy_hidden = jax.nn.silu(policy_pre).astype(jnp.bfloat16)
    value_hidden = jax.nn.silu(value_pre).astype(jnp.bfloat16)
    logits = jnp.dot(policy_hidden, policy_out, preferred_element_type=jnp.float32)
    value = jnp.dot(value_hidden, value_out, preferred_element_type=jnp.float32)
    top_logit = jnp.max(logits, axis=1, keepdims=True)
    log_total = top_logit[:, 0] + jnp.log(jnp.sum(jnp.exp(logits - top_logit), axis=1))
    target_onehot = (targets[:, None] == jnp.arange(action_count, dtype=jnp.int32)[None, :]).astype(
        jnp.float32
    )
    picked = jnp.sum(logits * target_onehot, axis=1)
    errors = value - returns
    local_sums = jnp.stack([jnp.sum(log_total - picked), 0.5 * jnp.sum(errors * errors)])
    losses = lax.psum(local_sums, "wide") / total_rows
    factor = total_rows ** (-0.5)
    dlogits = ((jnp.exp(logits - log_total[:, None]) - target_onehot) * factor).astype(jnp.bfloat16)
    dvalue = (errors * factor).astype(jnp.bfloat16)
    local_policy_out = jnp.dot(policy_hidden.T, dlogits, preferred_element_type=jnp.float32)
    local_value_out = jnp.dot(dvalue, value_hidden, preferred_element_type=jnp.float32)
    policy_dpre = (
        jnp.dot(dlogits, policy_out.T, preferred_element_type=jnp.float32) * silu_slope(policy_pre)
    ).astype(jnp.bfloat16)
    value_dpre = (
        dvalue.astype(jnp.float32)[:, None]
        * value_out.astype(jnp.float32)[None, :]
        * silu_slope(value_pre)
    ).astype(jnp.bfloat16)
    local_policy_in = jnp.dot(heads_in.T, policy_dpre, preferred_element_type=jnp.float32)
    local_value_in = jnp.dot(heads_in.T, value_dpre, preferred_element_type=jnp.float32)
    policy_in_grad, value_in_grad, policy_out_grad, value_out_grad = lax.psum(
        (local_policy_in, local_value_in, local_policy_out, local_value_out), "wide"
    )
    policy_in_grad = policy_in_grad.astype(jnp.bfloat16)
    value_in_grad = value_in_grad.astype(jnp.bfloat16)
    return (
        new_latent,
        losses,
        policy_in_grad,
        value_in_grad,
        policy_out_grad.astype(jnp.bfloat16),
        value_out_grad.astype(jnp.bfloat16),
    )


def solution(mesh):
    placed = (
        P("wide", "narrow"),
        P("wide"),
        P(None, "narrow"),
        P("narrow"),
        P(None, "narrow"),
        P(None, "narrow"),
        P(None, "narrow"),
        P(None, "narrow"),
        P("wide", None, "narrow"),
        P("wide", None, "narrow"),
        P("narrow"),
        P("narrow", None),
        P("narrow", None),
        P(),
        P(),
        P("wide"),
        P("wide"),
    )
    return jax.shard_map(
        per_device,
        mesh=mesh,
        in_specs=placed,
        out_specs=(P("wide", "narrow"), P(), P("narrow", None), P("narrow", None), P(), P()),
        check_vma=False,
    )
```

profile of v0, /device:TPU:24, one launch (start us, length us, event | category | flops | bytes accessed | tf_op | source)
XLA Modules:
  0.0 368.1 jit_solution(16743200332388699977)
XLA Ops:
  7.2 1.5 multiply_reduce_fusion.1
  8.8 10.5 %psum.63 = f32[256]{0:T(256)S(1)} all-reduce(f32[256]{0:T(256)S(1)} %get-tuple-element.24), channel_id=1, replica_groups=mesh['wide'=32,'narrow'=8] {'narrow'}, use_global_device_ids=true, to_apply=%region_1.0 | all-reduce | flops 256 | bytes 2048 | tf_op jit(solution)/shard_map/psum | solution.py:50
  19.2 1.5 multiply_convert_fusion.4
  20.8 31.3 %all-gather.3.cloned.1.call-done = bf16[256,4096]{1,0:T(8,128)(2,1)} async-done(((bf16[256,512]{1,0:T(8,128)(2,1)}), bf16[256,4096]{1,0:T(8,128)(2,1)}) %all-gather.3.cloned.1.call-update) | async-done | bytes 2097168 | tf_op jit(solution)/shard_map/all_gather | solution.py:53
  52.1 2.9 convolution_convert_fusion.2
  55.1 2.9 fusion.6
  58.2 0.4 multiply_reduce_fusion.2
  58.6 3.0 fusion.5
  61.6 0.8 reshape.74
  62.5 0.4 fusion.29
  62.8 0.3 fusion.7
  63.2 0.2 copy-done.3
  63.4 0.2 copy-done.8
  63.6 0.4 fusion.4
  64.1 0.7 copy.66
  64.9 26.7 %all-gather.5.cloned.1.call-done = bf16[256,2048]{1,0:T(8,128)(2,1)} async-done(((bf16[256,256]{1,0:T(8,128)(2,1)}), bf16[256,2048]{1,0:T(8,128)(2,1)}) %all-gather.5.cloned.1.call-update) | async-done | bytes 1048592 | tf_op jit(solution)/shard_map/all_gather | solution.py:81
  91.5 2.0 multiply_reduce_fusion
  93.5 11.1 %psum.64 = f32[256]{0:T(256)S(1)} all-reduce(f32[256]{0:T(256)S(1)} %get-tuple-element.28), channel_id=1, replica_groups=mesh['wide'=32,'narrow'=8] {'narrow'}, use_global_device_ids=true, to_apply=%region_6.0 | all-reduce | flops 256 | bytes 2048 | tf_op jit(solution)/shard_map/psum | solution.py:87
  104.6 0.7 multiply_convert_fusion.3
  105.4 2.1 fusion.32
  107.5 2.2 fusion.31
  109.7 68.2 %all-reduce.5.cloned.1.call-done = (f32[256,512]{1,0:T(8,128)}, f32[256,512]{1,0:T(8,128)}) async-done(((f32[256,512]{1,0:T(8,128)}, f32[256,512]{1,0:T(8,128)}), (f32[256,512]{1,0:T(8,128)}, f32[256,512]{1,0:T(8,128)})) %all-reduce.5.cloned.1.call-update) | async-done | bytes 1048592 | tf_op jit(solution)/shard_map/psum | solution.py:90
  178.0 1.5 multiply_convert_fusion.1
  179.5 0.3 fusion.30
  179.9 0.6 subtract_reduce_fusion
  180.5 0.3 fusion.27
  180.8 2.7 fusion.3
  183.6 0.6 fusion.28
  185.1 0.7 pad_maximum_fusion
  185.8 2.6 fusion.16
  188.4 172.7 %all-reduce.6 = (f32[2]{0:T(128)S(1)}, bf16[512,512]{1,0:T(8,128)(2,1)}, bf16[512,512]{1,0:T(8,128)(2,1)}, bf16[512,256]{1,0:T(8,128)(2,1)}, bf16[512]{0:T(512)(128)(2,1)}) all-reduce(f32[2]{0:T(128)S(1)} %pad_maximum_fusion, f32[512,512]{1,0:T(8,128)} %fusion.3, ...), channel_id=1, replica_groups=mesh['wide'=32,'narrow'=8] {'wide'}, use_global_device_ids=true, to_apply=%region_14.15 | all-reduce | flops 655874 | bytes 3935248 | tf_op jit(solution)/shard_map/psum | solution.py:109
  361.1 0.5 broadcast_multiply_fusion
  (36 shorter events, 1.0 us)
Async XLA Ops:
  7.2 84.4 %copy-start = (bf16[2048,512]{1,0:T(8,128)(2,1)S(1)}, bf16[2048,512]{1,0:T(8,128)(2,1)}, u32[]{:S(2)}) copy-start(bf16[2048,512]{1,0:T(8,128)(2,1)} %param.24) | copy-start | bytes 6291460
  7.2 44.9 %all-gather.3.cloned.1.call-start = ((), (), s32[]{:S(2)}) async-start(), calls=%async_computation | async-start | bytes 2359296 | tf_op jit(solution)/shard_map/all_gather | solution.py:53
  20.8 70.8 %all-gather.5.cloned.1.call-start = ((), (), s32[]{:S(2)}) async-start(), calls=%async_computation.1 | async-start | bytes 1179648 | tf_op jit(solution)/shard_map/all_gather | solution.py:81
  58.6 3.8 %copy-start.1 = (bf16[2,512,256]{2,1,0:T(8,128)(2,1)S(1)}, bf16[2,512,256]{2,1,0:T(8,128)(2,1)}, u32[]{:S(2)}) copy-start(bf16[2,512,256]{2,1,0:T(8,128)(2,1)} %param.25) | copy-start | bytes 1572868
  62.4 1.0 copy-start.3
  62.4 1.1 copy-start.8
  64.8 39.8 %copy-start.6 = (f32[512]{0:T(512)S(1)}, f32[512]{0:T(512)}, u32[]{:S(2)}) copy-start(f32[512]{0:T(512)} %param.27) | copy-start | bytes 6148
  64.8 113.2 %all-reduce.5.cloned.1.call-start = ((), (), s32[]{:S(2)}) async-start(), calls=%async_computation.2 | async-start | bytes 2097152 | tf_op jit(solution)/shard_map/psum | solution.py:90
  105.4 4.4 %copy-start.4 = (bf16[512]{0:T(512)(128)(2,1)S(1)}, bf16[512]{0:T(512)(128)(2,1)}, u32[]{:S(2)}) copy-start(bf16[512]{0:T(512)(128)(2,1)} %param.31) | copy-start | bytes 3076
  107.5 72.0 %copy-start.2 = (bf16[512,256]{1,0:T(8,128)(2,1)S(1)}, bf16[512,256]{1,0:T(8,128)(2,1)}, u32[]{:S(2)}) copy-start(bf16[512,256]{1,0:T(8,128)(2,1)} %param.30) | copy-start | bytes 786436
  107.5 72.3 %copy-start.5 = (s32[256]{0:T(256)S(1)}, s32[256]{0:T(256)}, u32[]{:S(2)}) copy-start(s32[256]{0:T(256)} %param.32) | copy-start | bytes 3076
  180.7 2.9 copy-start.7
Sparse Core Ops, SparseCore 0:
  20.9 31.1 all-gather.2
  64.9 26.5 all-gather.4
  109.8 68.0 all-reduce.4
where the time goes:
time: 369 us; the launch traced here: 368 us
  blocking collectives  194 us (53%)
  waiting for transfers between devices  126 us (34%)
  matrix products  23.6 us (6%)
  between operations  14.6 us (4%)
  other arithmetic  7.01 us (2%)
    psum x1, blocking collectives, per_device(): losses = lax.psum(local_sums, 'wide') / total_rows  173 us
    psum x1, waiting for transfers between devices, per_device(): lax.psum((jnp.dot(heads_in, policy_in, preferred_element_type=jnp.float32...  68.2 us
    all_gather x1, waiting for transfers between devices, per_device(): segment = lax.all_gather(normed, 'narrow', axis=1, tiled=True)  31.3 us
    all_gather x1, waiting for transfers between devices, per_device(): lax.all_gather(attended, 'narrow', axis=1, tiled=True)  26.7 us
    psum x1, blocking collectives, per_device(): squares_two = lax.psum(jnp.sum(state * state, axis=1), 'narrow')  11.1 us
    psum x1, blocking collectives, per_device(): squares = lax.psum(jnp.sum(tokens * tokens, axis=1), 'narrow')  10.5 us
    dot_general x3, matrix products, per_device(): jnp.dot(segment, matrix, preferred_element_type=jnp.float32)  8.85 us
  transfers between devices with their start and end apart: 3, of which 3 were waited for; matrix products, arithmetic and copies ran while one was open for 0% of the time, Pallas kernels for 0%

commit v1 on v0

v1 whole, which is shorter than its diff:
```python
import functools

import jax
import jax.numpy as jnp
from jax import lax
from jax.experimental import pallas as pl
from jax.experimental.pallas import tpu as pltpu
from jax.sharding import PartitionSpec as P

HD = 128
EPSILON = 1e-05
X, Y, Z = 4, 4, 8
NARROW = 2 * Y
MESH = pl.DeviceIdType.MESH
F32, BF16 = jnp.float32, jnp.bfloat16
COPIES = 200


def nt_dot(left, right):
    return lax.dot_general(left, right, (((1,), (1,)), ((), ())), preferred_element_type=F32)


def dot(left, right):
    return jnp.dot(left, right, preferred_element_type=F32)


def kernel(
    latent_in,
    actions_in,
    table_in,
    gain1_in,
    w_query_in,
    w_key_in,
    w_value_in,
    w_out_in,
    keys_in,
    values_in,
    gain2_in,
    policy_in_in,
    value_in_in,
    policy_out_in,
    value_out_in,
    targets_in,
    returns_in,
    latent_out,
    grads_out,
    policy_out_grad,
    misc_out,
    latent,
    actions,
    table,
    gain1,
    w_qkv,
    w_out,
    keys,
    values,
    gain2,
    heads_w,
    policy_out,
    value_out,
    targets,
    returns,
    normed,
    squares,
    tokens,
    qkv,
    attended,
    gained_t,
    pre_send,
    pre_recv,
    onehot,
    returns_col,
    dpre_send,
    dpre_recv,
    factor_send,
    factor_recv,
    misc_send,
    misc_recv,
    grad_f32,
    grad_send,
    grad_recv,
    block_f32,
    block_send,
    block_recv,
    block_mid,
    block_recv_z,
    misc_x,
    misc_z,
    load_sem,
    send_sem,
    recv_sem,
):
    wide, narrow = lax.axis_index("wide"), lax.axis_index("narrow")
    x, z = wide // Z, lax.rem(wide, Z)
    y, c = narrow // 2, lax.rem(narrow, 2)
    scenes, branch, width = normed.shape[1:]
    total_rows = scenes * branch * X * Z
    full_width = width * NARROW

    def device(dx=0, dy=0, dz=0, dc=0):
        return (
            lax.rem(x + dx, X) * Z + lax.rem(z + dz, Z),
            lax.rem(y + dy, Y) * 2 + lax.rem(c + dc, 2),
        )

    plane = [(dx, dy, dc) for dx in (2, 1, 3, 0) for dy in (2, 1, 3, 0) for dc in (1, 0)]
    plane = [o for o in plane if o != (0, 0, 0)]
    z_steps = (4, 3, 5, 2, 6, 1, 7)
    x_steps = (2, 1, 3)
    y_steps = (2, 1, 3)
    barrier = pltpu.get_barrier_semaphore()
    partners = [device(dx, dy, 0, dc) for dx, dy, dc in plane] + [device(dz=d) for d in z_steps]
    for partner in partners:
        pl.semaphore_signal(barrier, inc=1, device_id=partner, device_id_type=MESH)

    loads = {}

    def load(name, source, target):
        copy = pltpu.make_async_copy(source, target, load_sem.at[len(loads)])
        copy.start()
        loads[name] = copy

    load("actions", actions_in, actions)
    load("table", table_in, table)
    load("latent", latent_in, latent)
    load("gain1", gain1_in, gain1)
    load("w_query", w_query_in, w_qkv.at[0])
    load("w_key", w_key_in, w_qkv.at[1])
    load("w_value", w_value_in, w_qkv.at[2])
    load("keys", keys_in, keys)
    load("values", values_in, values)
    load("w_out", w_out_in, w_out)
    load("gain2", gain2_in, gain2)
    load("policy_in", policy_in_in, heads_w.at[0])
    load("value_in", value_in_in, heads_w.at[1])
    load("policy_out", policy_out_in, policy_out)
    load("value_out", value_out_in, value_out)
    load("targets", targets_in, targets)
    load("returns", returns_in, returns)

    started = []

    def send(source, target, partner):
        i = len(started)
        copy = pltpu.make_async_remote_copy(
            src_ref=source,
            dst_ref=target,
            send_sem=send_sem.at[i],
            recv_sem=recv_sem.at[i],
            device_id=partner,
            device_id_type=MESH,
        )
        copy.start()
        started.append(copy)
        return copy

    for name in ("actions", "table", "latent", "gain1"):
        loads[name].wait()
    action_count = table.shape[0]
    action_ids = lax.broadcasted_iota(jnp.int32, (action_count, branch), 0)
    for s in range(scenes):
        chosen = (actions[s : s + 1, :] == action_ids).astype(F32).T.astype(BF16)
        token = latent[s].astype(F32) + dot(chosen, table[...])
        tokens[s] = token
        normed[narrow, s] = (token * gain1[...]).astype(BF16)
        square = token * token
        square = sum(square[:, i : i + 128] for i in range(0, width, 128))
        squares[narrow, s : s + 1, :] = jnp.sum(square.T, axis=0, keepdims=True)

    pl.semaphore_wait(barrier, len(partners))

    def gather_start(buffer, s):
        own = buffer.at[narrow, s]
        near = send(own, own, device(dc=1))
        far = [send(own, own, device(dy=d)) for d in y_steps]
        return near, far

    def gather_slots(buffer, s, near, far):
        yield narrow
        near.wait_recv()
        yield y * 2 + 1 - c
        passed = []
        for d, copy in zip(y_steps, far):
            slot = lax.rem(y - d + Y, Y) * 2 + c
            copy.wait_recv()
            passed.append(send(buffer.at[slot, s], buffer.at[slot, s], device(dc=1)))
            yield slot
        for d, copy in zip(y_steps, passed):
            copy.wait_recv()
            yield lax.rem(y - d + Y, Y) * 2 + 1 - c

    gathers = [gather_start(normed, 0)]
    square_copies = [
        send(squares.at[narrow], squares.at[narrow], device(dy=dy, dc=dc))
        for dx, dy, dc in plane
        if dx == 0
    ]
    gathers.append(gather_start(normed, 1))

    loads["targets"].wait()
    loads["returns"].wait()
    for s in range(scenes):
        onehot[s] = (targets[s : s + 1, :] == action_ids).astype(F32).T
        returns_col[s] = jnp.broadcast_to(returns[s : s + 1, :], (128, branch)).T

    for name in ("w_query", "w_key", "w_value", "keys", "values"):
        loads[name].wait()
    scaling = HD ** (-0.5)
    heads_local = w_qkv.shape[2] // HD
    attended_copies = []
    for s in range(scenes):
        first = True
        for slot in gather_slots(normed, s, *gathers[s]):
            rows = normed[slot, s]
            for i in range(3):
                product = dot(rows, w_qkv[i, pl.ds(pl.multiple_of(slot * width, width), width), :])
                if first:
                    qkv[i] = product
                else:
                    qkv[i] += product
            first = False
        if s == 0:
            for copy in square_copies:
                copy.wait_recv()
        total = jnp.sum(squares[:, s : s + 1, :], axis=0)
        inverse = lax.rsqrt(total / full_width + EPSILON)
        inverse = jnp.broadcast_to(inverse, (128, branch)).T
        for h in range(heads_local):
            cols = slice(h * HD, (h + 1) * HD)
            query, key_new, value_new = ((qkv[i, :, cols] * inverse).astype(BF16) for i in range(3))
            scores = nt_dot(query, keys[s, :, cols]) * scaling
            own_score = (
                jnp.sum(query.astype(F32) * key_new.astype(F32), axis=1, keepdims=True) * scaling
            )
            highest = jnp.maximum(jnp.max(scores, axis=1, keepdims=True), own_score)
            expd = jnp.exp(scores - highest)
            own_exp = jnp.exp(own_score - highest)
            share = 1.0 / (jnp.sum(expd, axis=1, keepdims=True) + own_exp)
            weights = (expd * share).astype(BF16)
            own_weight = (own_exp * share).astype(BF16).astype(F32)
            mixed = dot(weights, values[s, :, cols]) + own_weight * value_new.astype(F32)
            attended[narrow, s, :, cols] = mixed.astype(BF16)
        attended_copies.append(gather_start(attended, s))

    for name in ("w_out", "gain2", "policy_in", "value_in"):
        loads[name].wait()
    heads_width = heads_w.shape[2]
    both = 2 * heads_width
    depth = attended.shape[3]
    share_rows = branch // NARROW
    my_rows = pl.ds(pl.multiple_of(narrow * share_rows, share_rows), share_rows)
    pre_copies, state_copies = [], []
    for s in range(scenes):
        for slot in gather_slots(attended, s, *attended_copies[s]):
            tokens[s] += dot(
                attended[slot, s], w_out[pl.ds(pl.multiple_of(slot * depth, depth), depth), :]
            )
        state = tokens[s]
        gained = state * gain2[...]
        gained_b = gained.astype(BF16)
        for i in range(2):
            pre_send[s, :, i * heads_width : (i + 1) * heads_width] = dot(
                gained_b, heads_w[i]
            ).astype(BF16)
        square = jnp.sum(state * state, axis=1, keepdims=True)
        high = square.astype(BF16)
        low = (square - high.astype(F32)).astype(BF16)
        lane = lax.broadcasted_iota(jnp.int32, (branch, 128), 1)
        pre_send[s, :, both:] = jnp.where(lane < 64, high.astype(F32), low.astype(F32)).astype(BF16)
        copies = []
        for dx, dy, dc in plane:
            if dx == 0:
                partner = device(dy=dy, dc=dc)
                rows = pl.ds(pl.multiple_of(partner[1] * share_rows, share_rows), share_rows)
                copies.append(send(pre_send.at[s, rows], pre_recv.at[narrow, s], partner))
        pre_copies.append(copies)
        pre_recv[narrow, s] = pre_send[s, my_rows, :]
        latent_out[s] = state.astype(BF16)
        gained_t[x, s] = gained.T.astype(BF16)
        state_copies.append(
            [send(gained_t.at[x, s], gained_t.at[x, s], device(dx=d)) for d in x_steps]
        )

    loads["policy_out"].wait()
    loads["value_out"].wait()
    for copies in pre_copies:
        for copy in copies:
            copy.wait_recv()
    sums = jnp.concatenate(
        [sum(pre_recv[i, s].astype(F32) for i in range(NARROW)) for s in range(scenes)], axis=0
    )
    square = sums[:, both : both + 1] + sums[:, both + 64 : both + 65]
    inverse = lax.rsqrt(square / full_width + EPSILON)
    pre = sums[:, :both] * inverse
    sigma = 1.0 / (1.0 + jnp.exp(-pre))
    hidden = (pre * sigma).astype(BF16)
    slope = sigma * (1.0 + pre * (1.0 - sigma))
    policy_hidden, value_hidden = hidden[:, :heads_width], hidden[:, heads_width:].astype(F32)
    logits = dot(policy_hidden, policy_out[...])
    value = jnp.sum(value_hidden * value_out[...], axis=1, keepdims=True)
    top = jnp.max(logits, axis=1, keepdims=True)
    log_total = top + jnp.log(jnp.sum(jnp.exp(logits - top), axis=1, keepdims=True))
    target = jnp.concatenate([onehot[s, my_rows, :] for s in range(scenes)], axis=0)
    wanted = jnp.concatenate([returns_col[s, my_rows, :] for s in range(scenes)], axis=0)
    picked = jnp.sum(logits * target, axis=1, keepdims=True)
    errors = value - wanted[:, 0:1]
    factor = total_rows ** (-0.5)
    dlogits = ((jnp.exp(logits - log_total) - target) * factor).astype(BF16)
    dvalue = (errors * factor).astype(BF16).astype(F32)
    dhidden = nt_dot(dlogits, policy_out[...])
    dpre_policy = (dhidden * slope[:, :heads_width] * inverse).astype(BF16)
    dpre_value = (dvalue * value_out[...] * slope[:, heads_width:] * inverse).astype(BF16)
    dpre = jnp.concatenate([dpre_policy, dpre_value], axis=1)
    cols = both // X
    for i in range(X):
        for s in range(scenes):
            dpre_send[i, s] = dpre[s * share_rows : (s + 1) * share_rows, i * cols : (i + 1) * cols]
    dpre_recv[x, :, my_rows, :] = dpre_send[x]
    dpre_copies = []
    for dx, dy, dc in plane:
        dpre_copies.append(
            send(
                dpre_send.at[lax.rem(x + dx, X)],
                dpre_recv.at[x, :, my_rows, :],
                device(dx=dx, dy=dy, dc=dc),
            )
        )

    block = heads_width // Y
    lanes = lax.broadcasted_iota(jnp.int32, (1, 128), 1)
    sum_policy = jnp.sum(log_total - picked, axis=0, keepdims=True)
    sum_value = 0.5 * jnp.sum(errors * errors, axis=0, keepdims=True)
    loss_row = jnp.where(lanes == 0, sum_policy, jnp.where(lanes == 1, sum_value, 0.0))
    value_row = jnp.sum(dvalue * value_hidden, axis=0, keepdims=True)
    for i in range(Y):
        for j in range(2):
            factor_send[2 * i + j, :, :block] = policy_hidden[:, i * block : (i + 1) * block]
            factor_send[2 * i + j, :, block:] = dlogits[:, j * 128 : (j + 1) * 128]
        misc_send[i] = jnp.concatenate(
            [value_row[:, i * block : (i + 1) * block], loss_row, jnp.zeros((6, 128), F32)], axis=0
        )
    factor_recv[narrow] = factor_send[narrow]
    misc_recv[narrow] = misc_send[y]
    factor_copies = []
    for dx, dy, dc in plane:
        if dx == 0:
            partner = device(dy=dy, dc=dc)
            factor_copies.append(send(factor_send.at[partner[1]], factor_recv.at[narrow], partner))
            factor_copies.append(
                send(misc_send.at[lax.rem(y + dy, Y)], misc_recv.at[narrow], partner)
            )

    for copies in state_copies:
        for copy in copies:
            copy.wait_recv()
    for copy in dpre_copies:
        copy.wait_recv()
    grad = None
    for i in range(X):
        for s in range(scenes):
            product = dot(gained_t[i, s], dpre_recv[i, s])
            grad = product if grad is None else grad + product
    grad_f32[...] = grad
    grad_send[...] = grad.astype(BF16)
    grad_rows = width // Z
    grad_copies = []
    for d in z_steps:
        rows = pl.ds(pl.multiple_of(lax.rem(z + d, Z) * grad_rows, grad_rows), grad_rows)
        grad_copies.append(send(grad_send.at[rows], grad_recv.at[d - 1], device(dz=d)))

    for copy in factor_copies:
        copy.wait_recv()
    left = jnp.concatenate([factor_recv[i, :, :block] for i in range(NARROW)], axis=0)
    right = jnp.concatenate([factor_recv[i, :, block:] for i in range(NARROW)], axis=0)
    part = dot(left.astype(F32).T.astype(BF16), right)
    block_f32[...] = part
    block_send[...] = part.astype(BF16)
    misc_x[0] = sum(misc_recv[i] for i in range(NARROW))
    block_rows = block // X
    block_copies = []
    for d in x_steps:
        rows = pl.ds(pl.multiple_of(lax.rem(x + d, X) * block_rows, block_rows), block_rows)
        block_copies.append(send(block_send.at[rows], block_recv.at[d - 1], device(dx=d)))
        block_copies.append(send(misc_x.at[0], misc_x.at[d], device(dx=d)))

    for copy in grad_copies:
        copy.wait_recv()
    my_grad = pl.ds(pl.multiple_of(z * grad_rows, grad_rows), grad_rows)
    my_cols = pl.ds(pl.multiple_of(lax.rem(x, 2) * cols, cols), cols)
    reduced = grad_f32[my_grad, :] + sum(grad_recv[i].astype(F32) for i in range(Z - 1))
    grads_out[x // 2, my_grad, my_cols] = reduced.astype(BF16)

    def spread(rows, **step):
        place = grads_out.at[x // 2, rows, my_cols]
        return send(place, place, device(**step))

    along_z = [spread(my_grad, dz=d) for d in z_steps]
    along_x = [spread(my_grad, dx=d) for d in x_steps]

    for copy in block_copies:
        copy.wait_recv()
    my_block = pl.ds(pl.multiple_of(x * block_rows, block_rows), block_rows)
    reduced = block_f32[my_block, :] + sum(block_recv[i].astype(F32) for i in range(X - 1))
    block_mid[...] = reduced.astype(BF16)
    misc_z[0] = sum(misc_x[i] for i in range(X))
    block_copies = []
    for d in z_steps:
        block_copies.append(send(block_mid, block_recv_z.at[d - 1], device(dz=d)))
        block_copies.append(send(misc_z.at[0], misc_z.at[d], device(dz=d)))

    def forward(d, copy):
        copy.wait_recv()
        rows = pl.ds(pl.multiple_of(lax.rem(z - d + Z, Z) * grad_rows, grad_rows), grad_rows)
        along_x.extend(spread(rows, dx=e) for e in x_steps)

    for d, copy in list(zip(z_steps, along_z))[::-1][:5]:
        forward(d, copy)

    for copy in block_copies:
        copy.wait_recv()
    reduced = reduced + sum(block_recv_z[i].astype(F32) for i in range(Z - 1))
    block_cols = pl.ds(pl.multiple_of(c * 128, 128), 128)
    place = policy_out_grad.at[
        pl.ds(pl.multiple_of(y * block + x * block_rows, block_rows), block_rows), block_cols
    ]
    place[...] = reduced.astype(BF16)
    block_copies = [send(place, place, device(dx=d)) for d in x_steps]
    misc_out[y] = sum(misc_z[i] for i in range(Z))
    misc_copies = [send(misc_out.at[y], misc_out.at[y], device(dy=d)) for d in y_steps]

    for d, copy in list(zip(z_steps, along_z))[::-1][5:]:
        forward(d, copy)

    for copy in block_copies:
        copy.wait_recv()
    place = policy_out_grad.at[pl.ds(pl.multiple_of(y * block, block), block), block_cols]
    block_copies = [send(place, place, device(dy=dy, dc=dc)) for dx, dy, dc in plane if dx == 0]

    for copy in misc_copies + along_x + block_copies:
        copy.wait_recv()
    for copy in started:
        copy.wait_send()


def per_device(
    latent,
    actions,
    action_table,
    norm1_gain,
    w_query,
    w_key,
    w_value,
    w_out,
    key_cache,
    value_cache,
    norm2_gain,
    policy_in,
    value_in,
    policy_out,
    value_out,
    targets,
    returns,
):
    rows, width = latent.shape
    scenes = key_cache.shape[0]
    branch = rows // scenes
    heads_width = policy_in.shape[1]
    features = w_query.shape[1]
    share = branch // NARROW
    block = heads_width // Y
    cols = 2 * heads_width // X
    total_rows = rows * X * Z
    vmem = pltpu.VMEM
    operands = (
        latent.reshape(scenes, branch, width),
        actions.reshape(scenes, branch),
        action_table,
        norm1_gain.reshape(1, width),
        w_query,
        w_key,
        w_value,
        w_out,
        key_cache,
        value_cache,
        norm2_gain.reshape(1, width),
        policy_in,
        value_in,
        policy_out,
        value_out.astype(F32).reshape(1, heads_width),
        targets.reshape(scenes, branch),
        returns.reshape(scenes, branch),
    )
    scratch = [
        vmem((scenes, branch, width), BF16),
        vmem((scenes, branch), jnp.int32),
        vmem(action_table.shape, BF16),
        vmem((1, width), F32),
        vmem((3,) + w_query.shape, BF16),
        vmem(w_out.shape, BF16),
        vmem(key_cache.shape, BF16),
        vmem(value_cache.shape, BF16),
        vmem((1, width), F32),
        vmem((2,) + policy_in.shape, BF16),
        vmem(policy_out.shape, BF16),
        vmem((1, heads_width), F32),
        vmem((scenes, branch), jnp.int32),
        vmem((scenes, branch), F32),
        vmem((NARROW, scenes, branch, width), BF16),
        vmem((NARROW, 8, branch), F32),
        vmem((scenes, branch, width), F32),
        vmem((3, branch, features), F32),
        vmem((NARROW, scenes, branch, features), BF16),
        vmem((X, scenes, width, branch), BF16),
        vmem((scenes, branch, 2 * heads_width + 128), BF16),
        vmem((NARROW, scenes, share, 2 * heads_width + 128), BF16),
        vmem((scenes, branch, policy_out.shape[1]), F32),
        vmem((scenes, branch, 128), F32),
        vmem((X, scenes, share, cols), BF16),
        vmem((X, scenes, branch, cols), BF16),
        vmem((NARROW, scenes * share, block + 128), BF16),
        vmem((NARROW, scenes * share, block + 128), BF16),
        vmem((Y, 8, 128), F32),
        vmem((NARROW, 8, 128), F32),
        vmem((width, cols), F32),
        vmem((width, cols), BF16),
        vmem((Z - 1, width // Z, cols), BF16),
        vmem((block, 128), F32),
        vmem((block, 128), BF16),
        vmem((X - 1, block // X, 128), BF16),
        vmem((block // X, 128), BF16),
        vmem((Z - 1, block // X, 128), BF16),
        vmem((X, 8, 128), F32),
        vmem((Z, 8, 128), F32),
        pltpu.SemaphoreType.DMA((len(operands),)),
        pltpu.SemaphoreType.DMA((COPIES,)),
        pltpu.SemaphoreType.DMA((COPIES,)),
    ]
    new_latent, grads, policy_out_grad, misc = pl.pallas_call(
        kernel,
        name="imagine",
        out_shape=(
            jax.ShapeDtypeStruct((scenes, branch, width), BF16),
            jax.ShapeDtypeStruct((2, width, heads_width), BF16),
            jax.ShapeDtypeStruct(policy_out.shape, BF16),
            jax.ShapeDtypeStruct((Y, 8, 128), F32),
        ),
        in_specs=[pl.BlockSpec(memory_space=pl.ANY)] * len(operands),
        out_specs=[pl.BlockSpec(memory_space=pltpu.VMEM)] * 4,
        scratch_shapes=scratch,
        compiler_params=pltpu.CompilerParams(
            collective_id=0, has_side_effects=True, vmem_limit_bytes=60 * 2**20
        ),
    )(*operands)
    return (
        new_latent.reshape(rows, width),
        misc[0, 1, :2] / total_rows,
        grads[0],
        grads[1],
        policy_out_grad,
        misc[:, 0, :].reshape(heads_width).astype(BF16),
    )


def solution(mesh):
    placed = (
        P("wide", "narrow"),
        P("wide"),
        P(None, "narrow"),
        P("narrow"),
        P(None, "narrow"),
        P(None, "narrow"),
        P(None, "narrow"),
        P(None, "narrow"),
        P("wide", None, "narrow"),
        P("wide", None, "narrow"),
        P("narrow"),
        P("narrow", None),
        P("narrow", None),
        P(),
        P(),
        P("wide"),
        P("wide"),
    )
    return jax.shard_map(
        per_device,
        mesh=mesh,
        in_specs=placed,
        out_specs=(P("wide", "narrow"), P(), P("narrow", None), P("narrow", None), P(), P()),
        check_vma=False,
    )
```

time: 369 us -> 92.9 us (0.25)
  the two profiles are of different devices: /device:TPU:24 before, /device:TPU:1 now
where the time goes in v1:
time: 92.9 us; the launch traced here: 92.7 us
  Pallas kernels  84.6 us (91%)
  local copies, waits for them, and re-layouts  4.94 us (5%)
  other arithmetic  2.5 us (3%)
    pallas_call x1, Pallas kernels, per_device(): pl.pallas_call(kernel, name='imagine', out_shape=(jax.ShapeDtypeStruct((s...  84.6 us
    squeeze x1, local copies, waits for them, and re-layouts, per_device(): grads[1]  2.23 us

profile of v1, /device:TPU:1, one launch (start us, length us, event | category | flops | bytes accessed | tf_op | source)
XLA Modules:
  0.0 92.7 jit_solution(9580428666789943269)
XLA Ops:
  0.6 1.3 %reshape.50 = f32[512]{0:T(512)} convert(bf16[512]{0:T(512)(128)(2,1)} %param.31) | non-fusion elementwise | flops 512 | bytes 3072 | tf_op jit(solution)/shard_map/reshape | solution.py:489
  1.9 84.6 %imagine.1 = (bf16[2,128,512]{2,1,0:T(8,128)(2,1)}, bf16[2,512,512]{2,1,0:T(8,128)(2,1)}, bf16[512,256]{1,0:T(8,128)(2,1)}, f32[4,8,128]{2,1,0:T(8,128)}) custom-call(bf16[2,128,512]{2,1,0:T(8,128)(2,1)} %bitcast.15, s32[2,128]{1,0:T(2,128)} %bitcast.20, bf16[256,512]{1,0:T(8,128)(2,1)} %table_in.1, f32[1,512]{1,0:T(1,128)} %bitcast.18, ...), custom_call_target="tpu_custom_call" | custom-call | tf_op jit(solution)/shard_map/imagine/pallas_call | solution.py:538
  86.5 0.0 copy-start.1
  86.5 0.0 copy-start
  86.5 1.2 %multiply_bitcast_fusion = f32[2]{0:T(128)} fusion(f32[4,8,128]{2,1,0:T(8,128)} %get-tuple-element.11), kind=kLoop, calls=%fused_computation.4 | loop fusion | flops 2 | bytes 16 | tf_op jit(solution)/shard_map/div | solution.py:556
  87.8 1.3 %fusion = bf16[4,128]{1,0:T(4,128)(2,1)} fusion(f32[4,8,128]{2,1,0:T(8,128)} %get-tuple-element.11), kind=kLoop, calls=%fused_computation.3 | loop fusion | bytes 2048 | tf_op jit(solution)/shard_map/slice | solution.py:560
  89.0 2.2 %slice_bitcast_fusion = (bf16[512,512]{1,0:T(8,128)(2,1)}, bf16[512,512]{1,0:T(8,128)(2,1)}) fusion(bf16[2,512,512]{2,1,0:T(8,128)(2,1)} %get-tuple-element.12), kind=kLoop, calls=%fused_computation | loop fusion | bytes 2097152 | tf_op jit(solution)/shard_map/squeeze | solution.py:558
  91.3 0.0 copy-done.1
  91.3 0.7 copy.25
  92.0 0.0 copy-done
  92.0 0.7 copy.26
Async XLA Ops:
  86.5 4.8 %copy-start.1 = (bf16[2,128,512]{2,1,0:T(8,128)(2,1)S(1)}, bf16[2,128,512]{2,1,0:T(8,128)(2,1)}, u32[]{:S(2)}) copy-start(bf16[2,128,512]{2,1,0:T(8,128)(2,1)} %get-tuple-element.10) | copy-start | bytes 786436
  86.5 5.5 %copy-start = (bf16[512,256]{1,0:T(8,128)(2,1)S(1)}, bf16[512,256]{1,0:T(8,128)(2,1)}, u32[]{:S(2)}) copy-start(bf16[512,256]{1,0:T(8,128)(2,1)} %get-tuple-element.26) | copy-start | bytes 786436

commit v2 on v1

--- a/solution.py
+++ b/solution.py
@@ -13,7 +13,7 @@
 NARROW = 2 * Y
 MESH = pl.DeviceIdType.MESH
 F32, BF16 = jnp.float32, jnp.bfloat16
-COPIES = 200
+COPIES = 256
 
 
 def nt_dot(left, right):
@@ -120,6 +120,11 @@
         copy.start()
         loads[name] = copy
 
+    def ready(*names):
+        for name in names:
+            loads[name].wait()
+            loads[name] = None
+
     load("actions", actions_in, actions)
     load("table", table_in, table)
     load("latent", latent_in, latent)
@@ -138,7 +143,7 @@
     load("targets", targets_in, targets)
     load("returns", returns_in, returns)
 
-    started = []
+    started, pending = [], {}
 
     def send(source, target, partner):
         i = len(started)
@@ -152,10 +157,21 @@
         )
         copy.start()
         started.append(copy)
+        pending[id(copy)] = copy
         return copy
 
-    for name in ("actions", "table", "latent", "gain1"):
-        loads[name].wait()
+    def arrive(*copies):
+        for copy in copies:
+            copy.wait_recv()
+            del pending[id(copy)]
+
+    def finish():
+        ready(*[name for name in loads if loads[name] is not None])
+        arrive(*list(pending.values()))
+        for copy in started:
+            copy.wait_send()
+
+    ready("actions", "table", "latent", "gain1")
     action_count = table.shape[0]
     action_ids = lax.broadcasted_iota(jnp.int32, (action_count, branch), 0)
     for s in range(scenes):
@@ -177,16 +193,16 @@
 
     def gather_slots(buffer, s, near, far):
         yield narrow
-        near.wait_recv()
+        arrive(near)
         yield y * 2 + 1 - c
         passed = []
         for d, copy in zip(y_steps, far):
             slot = lax.rem(y - d + Y, Y) * 2 + c
-            copy.wait_recv()
+            arrive(copy)
             passed.append(send(buffer.at[slot, s], buffer.at[slot, s], device(dc=1)))
             yield slot
         for d, copy in zip(y_steps, passed):
-            copy.wait_recv()
+            arrive(copy)
             yield lax.rem(y - d + Y, Y) * 2 + 1 - c
 
     gathers = [gather_start(normed, 0)]
@@ -197,14 +213,13 @@
     ]
     gathers.append(gather_start(normed, 1))
 
-    loads["targets"].wait()
-    loads["returns"].wait()
+    ready("targets")
+    ready("returns")
     for s in range(scenes):
         onehot[s] = (targets[s : s + 1, :] == action_ids).astype(F32).T
         returns_col[s] = jnp.broadcast_to(returns[s : s + 1, :], (128, branch)).T
 
-    for name in ("w_query", "w_key", "w_value", "keys", "values"):
-        loads[name].wait()
+    ready("w_query", "w_key", "w_value", "keys", "values")
     scaling = HD ** (-0.5)
     heads_local = w_qkv.shape[2] // HD
     attended_copies = []
@@ -220,8 +235,7 @@
                     qkv[i] += product
             first = False
         if s == 0:
-            for copy in square_copies:
-                copy.wait_recv()
+            arrive(*square_copies)
         total = jnp.sum(squares[:, s : s + 1, :], axis=0)
         inverse = lax.rsqrt(total / full_width + EPSILON)
         inverse = jnp.broadcast_to(inverse, (128, branch)).T
@@ -242,8 +256,7 @@
             attended[narrow, s, :, cols] = mixed.astype(BF16)
         attended_copies.append(gather_start(attended, s))
 
-    for name in ("w_out", "gain2", "policy_in", "value_in"):
-        loads[name].wait()
+    ready("w_out", "gain2", "policy_in", "value_in")
     heads_width = heads_w.shape[2]
     both = 2 * heads_width
     depth = attended.shape[3]
@@ -281,11 +294,10 @@
             [send(gained_t.at[x, s], gained_t.at[x, s], device(dx=d)) for d in x_steps]
         )
 
-    loads["policy_out"].wait()
-    loads["value_out"].wait()
+    ready("policy_out")
+    ready("value_out")
     for copies in pre_copies:
-        for copy in copies:
-            copy.wait_recv()
+        arrive(*copies)
     sums = jnp.concatenate(
         [sum(pre_recv[i, s].astype(F32) for i in range(NARROW)) for s in range(scenes)], axis=0
     )
@@ -297,7 +309,9 @@
     slope = sigma * (1.0 + pre * (1.0 - sigma))
     policy_hidden, value_hidden = hidden[:, :heads_width], hidden[:, heads_width:].astype(F32)
     logits = dot(policy_hidden, policy_out[...])
-    value = jnp.sum(value_hidden * value_out[...], axis=1, keepdims=True)
+    value_row = value_out[...].astype(F32)
+    value_row = jnp.concatenate([value_row[i : i + 1] for i in range(Y)], axis=1)
+    value = jnp.sum(value_hidden * value_row, axis=1, keepdims=True)
     top = jnp.max(logits, axis=1, keepdims=True)
     log_total = top + jnp.log(jnp.sum(jnp.exp(logits - top), axis=1, keepdims=True))
     target = jnp.concatenate([onehot[s, my_rows, :] for s in range(scenes)], axis=0)
@@ -309,7 +323,7 @@
     dvalue = (errors * factor).astype(BF16).astype(F32)
     dhidden = nt_dot(dlogits, policy_out[...])
     dpre_policy = (dhidden * slope[:, :heads_width] * inverse).astype(BF16)
-    dpre_value = (dvalue * value_out[...] * slope[:, heads_width:] * inverse).astype(BF16)
+    dpre_value = (dvalue * value_row * slope[:, heads_width:] * inverse).astype(BF16)
     dpre = jnp.concatenate([dpre_policy, dpre_value], axis=1)
     cols = both // X
     for i in range(X):
@@ -331,13 +345,13 @@
     sum_policy = jnp.sum(log_total - picked, axis=0, keepdims=True)
     sum_value = 0.5 * jnp.sum(errors * errors, axis=0, keepdims=True)
     loss_row = jnp.where(lanes == 0, sum_policy, jnp.where(lanes == 1, sum_value, 0.0))
-    value_row = jnp.sum(dvalue * value_hidden, axis=0, keepdims=True)
+    value_grad = jnp.sum(dvalue * value_hidden, axis=0, keepdims=True)
     for i in range(Y):
         for j in range(2):
             factor_send[2 * i + j, :, :block] = policy_hidden[:, i * block : (i + 1) * block]
             factor_send[2 * i + j, :, block:] = dlogits[:, j * 128 : (j + 1) * 128]
         misc_send[i] = jnp.concatenate(
-            [value_row[:, i * block : (i + 1) * block], loss_row, jnp.zeros((6, 128), F32)], axis=0
+            [value_grad[:, i * block : (i + 1) * block], loss_row, jnp.zeros((6, 128), F32)], axis=0
         )
     factor_recv[narrow] = factor_send[narrow]
     misc_recv[narrow] = misc_send[y]
@@ -351,25 +365,27 @@
             )
 
     for copies in state_copies:
-        for copy in copies:
-            copy.wait_recv()
-    for copy in dpre_copies:
-        copy.wait_recv()
+        arrive(*copies)
+    arrive(*dpre_copies)
     grad = None
     for i in range(X):
         for s in range(scenes):
             product = dot(gained_t[i, s], dpre_recv[i, s])
             grad = product if grad is None else grad + product
     grad_f32[...] = grad
-    grad_send[...] = grad.astype(BF16)
+    half = cols // 2
+    for i in range(2):
+        grad_send[i] = grad[:, i * half : (i + 1) * half].astype(BF16)
     grad_rows = width // Z
     grad_copies = []
-    for d in z_steps:
-        rows = pl.ds(pl.multiple_of(lax.rem(z + d, Z) * grad_rows, grad_rows), grad_rows)
-        grad_copies.append(send(grad_send.at[rows], grad_recv.at[d - 1], device(dz=d)))
-
-    for copy in factor_copies:
-        copy.wait_recv()
+    for i in range(2):
+        copies = []
+        for d in z_steps:
+            rows = pl.ds(pl.multiple_of(lax.rem(z + d, Z) * grad_rows, grad_rows), grad_rows)
+            copies.append(send(grad_send.at[i, rows], grad_recv.at[i, d - 1], device(dz=d)))
+        grad_copies.append(copies)
+
+    arrive(*factor_copies)
     left = jnp.concatenate([factor_recv[i, :, :block] for i in range(NARROW)], axis=0)
     right = jnp.concatenate([factor_recv[i, :, block:] for i in range(NARROW)], axis=0)
     part = dot(left.astype(F32).T.astype(BF16), right)
@@ -383,42 +399,41 @@
         block_copies.append(send(block_send.at[rows], block_recv.at[d - 1], device(dx=d)))
         block_copies.append(send(misc_x.at[0], misc_x.at[d], device(dx=d)))
 
-    for copy in grad_copies:
-        copy.wait_recv()
-    my_grad = pl.ds(pl.multiple_of(z * grad_rows, grad_rows), grad_rows)
-    my_cols = pl.ds(pl.multiple_of(lax.rem(x, 2) * cols, cols), cols)
-    reduced = grad_f32[my_grad, :] + sum(grad_recv[i].astype(F32) for i in range(Z - 1))
-    grads_out[x // 2, my_grad, my_cols] = reduced.astype(BF16)
-
-    def spread(rows, **step):
-        place = grads_out.at[x // 2, rows, my_cols]
-        return send(place, place, device(**step))
-
-    along_z = [spread(my_grad, dz=d) for d in z_steps]
-    along_x = [spread(my_grad, dx=d) for d in x_steps]
-
-    for copy in block_copies:
-        copy.wait_recv()
+    arrive(*block_copies)
     my_block = pl.ds(pl.multiple_of(x * block_rows, block_rows), block_rows)
-    reduced = block_f32[my_block, :] + sum(block_recv[i].astype(F32) for i in range(X - 1))
-    block_mid[...] = reduced.astype(BF16)
+    block_sum = block_f32[my_block, :] + sum(block_recv[i].astype(F32) for i in range(X - 1))
+    block_mid[...] = block_sum.astype(BF16)
     misc_z[0] = sum(misc_x[i] for i in range(X))
     block_copies = []
     for d in z_steps:
         block_copies.append(send(block_mid, block_recv_z.at[d - 1], device(dz=d)))
         block_copies.append(send(misc_z.at[0], misc_z.at[d], device(dz=d)))
 
-    def forward(d, copy):
-        copy.wait_recv()
-        rows = pl.ds(pl.multiple_of(lax.rem(z - d + Z, Z) * grad_rows, grad_rows), grad_rows)
-        along_x.extend(spread(rows, dx=e) for e in x_steps)
-
-    for d, copy in list(zip(z_steps, along_z))[::-1][:5]:
-        forward(d, copy)
-
-    for copy in block_copies:
-        copy.wait_recv()
-    reduced = reduced + sum(block_recv_z[i].astype(F32) for i in range(Z - 1))
+    my_grad = pl.ds(pl.multiple_of(z * grad_rows, grad_rows), grad_rows)
+
+    def spread(i, rows, **step):
+        my_cols = pl.ds(pl.multiple_of(lax.rem(x, 2) * cols + i * half, half), half)
+        place = grads_out.at[x // 2, rows, my_cols]
+        return send(place, place, device(**step))
+
+    along_z, along_x = [], []
+    for i in range(2):
+        arrive(*grad_copies[i])
+        reduced = grad_f32[my_grad, i * half : (i + 1) * half]
+        reduced = reduced + sum(grad_recv[i, j].astype(F32) for j in range(Z - 1))
+        my_cols = pl.ds(pl.multiple_of(lax.rem(x, 2) * cols + i * half, half), half)
+        grads_out[x // 2, my_grad, my_cols] = reduced.astype(BF16)
+        along_z.append({d: spread(i, my_grad, dz=d) for d in z_steps})
+        along_x.extend(spread(i, my_grad, dx=d) for d in x_steps)
+
+    def forward(i, *steps):
+        for d in steps:
+            arrive(along_z[i][d])
+            rows = pl.ds(pl.multiple_of(lax.rem(z - d + Z, Z) * grad_rows, grad_rows), grad_rows)
+            along_x.extend(spread(i, rows, dx=e) for e in x_steps)
+
+    arrive(*block_copies)
+    reduced = block_sum + sum(block_recv_z[i].astype(F32) for i in range(Z - 1))
     block_cols = pl.ds(pl.multiple_of(c * 128, 128), 128)
     place = policy_out_grad.at[
         pl.ds(pl.multiple_of(y * block + x * block_rows, block_rows), block_rows), block_cols
@@ -427,19 +442,54 @@
     block_copies = [send(place, place, device(dx=d)) for d in x_steps]
     misc_out[y] = sum(misc_z[i] for i in range(Z))
     misc_copies = [send(misc_out.at[y], misc_out.at[y], device(dy=d)) for d in y_steps]
-
-    for d, copy in list(zip(z_steps, along_z))[::-1][5:]:
-        forward(d, copy)
-
-    for copy in block_copies:
-        copy.wait_recv()
+    forward(0, 1, 7, 2, 6)
+    arrive(*block_copies)
     place = policy_out_grad.at[pl.ds(pl.multiple_of(y * block, block), block), block_cols]
     block_copies = [send(place, place, device(dy=dy, dc=dc)) for dx, dy, dc in plane if dx == 0]
-
-    for copy in misc_copies + along_x + block_copies:
-        copy.wait_recv()
-    for copy in started:
-        copy.wait_send()
+    forward(0, 3, 5, 4)
+    forward(1, 1, 7, 2, 6, 3, 5, 4)
+    finish()
+
+
+def deliver(
+    total_rows,
+    latent,
+    grads,
+    policy_out_grad,
+    misc,
+    latent_to,
+    policy_in_to,
+    value_in_to,
+    policy_out_to,
+    losses_to,
+    value_out_to,
+    losses,
+    value_out_grad,
+    sem,
+):
+    copies = [
+        pltpu.make_async_copy(source, target, sem.at[i])
+        for i, (source, target) in enumerate(
+            (
+                (grads.at[0], policy_in_to),
+                (grads.at[1], value_in_to),
+                (latent, latent_to),
+                (policy_out_grad, policy_out_to),
+                (losses, losses_to),
+                (value_out_grad, value_out_to),
+            )
+        )
+    ]
+    for copy in copies[:4]:
+        copy.start()
+    losses[...] = misc[0, 1:2, :2] * (1.0 / total_rows)
+    value_out_grad[...] = jnp.concatenate(
+        [misc[i, 0:1, :] for i in range(misc.shape[0])], axis=0
+    ).astype(BF16)
+    for copy in copies[4:]:
+        copy.start()
+    for copy in copies:
+        copy.wait()
 
 
 def per_device(
@@ -486,10 +536,11 @@
         policy_in,
         value_in,
         policy_out,
-        value_out.astype(F32).reshape(1, heads_width),
+        value_out.reshape(Y, 128),
         targets.reshape(scenes, branch),
         returns.reshape(scenes, branch),
     )
+    operands = [pltpu.with_memory_space_constraint(operand, pltpu.HBM) for operand in operands]
     scratch = [
         vmem((scenes, branch, width), BF16),
         vmem((scenes, branch), jnp.int32),
@@ -502,7 +553,7 @@
         vmem((1, width), F32),
         vmem((2,) + policy_in.shape, BF16),
         vmem(policy_out.shape, BF16),
-        vmem((1, heads_width), F32),
+        vmem((Y, 128), BF16),
         vmem((scenes, branch), jnp.int32),
         vmem((scenes, branch), F32),
         vmem((NARROW, scenes, branch, width), BF16),
@@ -522,8 +573,8 @@
         vmem((Y, 8, 128), F32),
         vmem((NARROW, 8, 128), F32),
         vmem((width, cols), F32),
-        vmem((width, cols), BF16),
-        vmem((Z - 1, width // Z, cols), BF16),
+        vmem((2, width, cols // 2), BF16),
+        vmem((2, Z - 1, width // Z, cols // 2), BF16),
         vmem((block, 128), F32),
         vmem((block, 128), BF16),
         vmem((X - 1, block // X, 128), BF16),
@@ -535,29 +586,49 @@
         pltpu.SemaphoreType.DMA((COPIES,)),
         pltpu.SemaphoreType.DMA((COPIES,)),
     ]
-    new_latent, grads, policy_out_grad, misc = pl.pallas_call(
+    results = pl.pallas_call(
         kernel,
         name="imagine",
         out_shape=(
-            jax.ShapeDtypeStruct((scenes, branch, width), BF16),
-            jax.ShapeDtypeStruct((2, width, heads_width), BF16),
-            jax.ShapeDtypeStruct(policy_out.shape, BF16),
-            jax.ShapeDtypeStruct((Y, 8, 128), F32),
+            vmem((scenes, branch, width), BF16),
+            vmem((2, width, heads_width), BF16),
+            vmem(policy_out.shape, BF16),
+            vmem((Y, 8, 128), F32),
         ),
-        in_specs=[pl.BlockSpec(memory_space=pl.ANY)] * len(operands),
+        in_specs=[pl.BlockSpec(memory_space=pltpu.HBM)] * len(operands),
         out_specs=[pl.BlockSpec(memory_space=pltpu.VMEM)] * 4,
         scratch_shapes=scratch,
         compiler_params=pltpu.CompilerParams(
-            collective_id=0, has_side_effects=True, vmem_limit_bytes=60 * 2**20
+            collective_id=0, has_side_effects=True, vmem_limit_bytes=40 * 2**20
         ),
     )(*operands)
+    new_latent, policy_in_grad, value_in_grad, policy_out_grad, losses, value_out_grad = pl.pallas_call(
+        functools.partial(deliver, total_rows),
+        name="deliver",
+        out_shape=(
+            jax.ShapeDtypeStruct((scenes, branch, width), BF16),
+            jax.ShapeDtypeStruct(policy_in.shape, BF16),
+            jax.ShapeDtypeStruct(value_in.shape, BF16),
+            jax.ShapeDtypeStruct(policy_out.shape, BF16),
+            jax.ShapeDtypeStruct((1, 2), F32),
+            jax.ShapeDtypeStruct((Y, 128), BF16),
+        ),
+        in_specs=[pl.BlockSpec(memory_space=pltpu.VMEM)] * 4,
+        out_specs=[pl.BlockSpec(memory_space=pltpu.HBM)] * 6,
+        scratch_shapes=[
+            vmem((1, 2), F32),
+            vmem((Y, 128), BF16),
+            pltpu.SemaphoreType.DMA((6,)),
+        ],
+        compiler_params=pltpu.CompilerParams(vmem_limit_bytes=8 * 2**20),
+    )(*[pltpu.with_memory_space_constraint(result, pltpu.VMEM) for result in results])
     return (
         new_latent.reshape(rows, width),
-        misc[0, 1, :2] / total_rows,
-        grads[0],
-        grads[1],
+        losses.reshape(2),
+        policy_in_grad,
+        value_in_grad,
         policy_out_grad,
-        misc[:, 0, :].reshape(heads_width).astype(BF16),
+        value_out_grad.reshape(heads_width),
     )
 
 

time: 92.9 us -> 79.4 us (0.85)
  Pallas kernels: 84.6 us -> 78.7 us
  local copies, waits for them, and re-layouts: 4.94 us -> 0 us
  other arithmetic: 2.5 us -> 0 us
    pallas_call x1 -> x2, Pallas kernels: 84.6 us -> 78.7 us  [the longest x1 77.5 us: per_device(): pl.pallas_call(kernel, name='imagine', out_shape=(vmem((scenes, branch, w...]
    squeeze x1 -> x0, local copies, waits for them, and re-layouts: 2.23 us -> none  [per_device(): grads[1]]
    unnamed x6 -> x0, local copies, waits for them, and re-layouts: 1.41 us -> none
    slice x1 -> x0, local copies, waits for them, and re-layouts: 1.3 us -> none  [per_device(): misc[:, 0, :].reshape(heads_width).astype(BF16)]
    reshape x1 -> x0, other arithmetic: 1.26 us -> none  [per_device(): value_out.astype(F32).reshape(1, heads_width)]
    div x1 -> x0, other arithmetic: 1.24 us -> none  [per_device(): misc[0, 1, :2] / total_rows]
where the time goes in v2:
time: 79.4 us
  Pallas kernels  78.7 us (99%)
    pallas_call x1, Pallas kernels, per_device(): pl.pallas_call(kernel, name='imagine', out_shape=(vmem((scenes, branch, w...  77.5 us

profile of v2, /device:TPU:1, one launch (start us, length us, event | category | flops | bytes accessed | tf_op | source)
XLA Modules:
  0.0 79.4 jit_solution(1454533331679633687)
XLA Ops:
  0.6 77.5 %imagine.1 = (bf16[2,128,512]{2,1,0:T(8,128)(2,1)S(1)}, bf16[2,512,512]{2,1,0:T(8,128)(2,1)S(1)}, bf16[512,256]{1,0:T(8,128)(2,1)S(1)}, f32[4,8,128]{2,1,0:T(8,128)S(1)}) custom-call(bf16[2,128,512]{2,1,0:T(8,128)(2,1)} %bitcast.10, s32[2,128]{1,0:T(2,128)} %bitcast.13, bf16[256,512]{1,0:T(8,128)(2,1)} %table_in.1, f32[1,512]{1,0:T(1,128)} %bitcast.11, ...), custom_call_target="tpu_custom_call" | custom-call | tf_op jit(solution)/shard_map/imagine/pallas_call | solution.py:589
  78.2 1.2 %deliver.1 = (bf16[2,128,512]{2,1,0:T(8,128)(2,1)}, bf16[512,512]{1,0:T(8,128)(2,1)}, bf16[512,512]{1,0:T(8,128)(2,1)}, bf16[512,256]{1,0:T(8,128)(2,1)}, f32[1,2]{1,0:T(1,128)}, /*index=5*/bf16[4,128]{1,0:T(4,128)(2,1)}) custom-call(bf16[2,128,512]{2,1,0:T(8,128)(2,1)S(1)} %get-tuple-element.16.latent, bf16[2,512,512]{2,1,0:T(8,128)(2,1)S(1)} %get-tuple-element.17.grads, ...), custom_call_target="tpu_custom_call" | custom-call | tf_op jit(solution)/shard_map/deliver/pallas_call | solution.py:605

commit v3 on v2

v3 whole, which is shorter than its diff:
```python
import functools

import jax
import jax.numpy as jnp
from jax import lax
from jax.experimental import pallas as pl
from jax.experimental.pallas import tpu as pltpu
from jax.sharding import PartitionSpec as P

HD = 128
EPSILON = 1e-05
X, Y, Z = 4, 4, 8
NARROW = 2 * Y
MESH = pl.DeviceIdType.MESH
F32, BF16 = jnp.float32, jnp.bfloat16
LOADS, SENDS, ARRIVALS = 14, 19, 75


def nt_dot(left, right):
    return lax.dot_general(left, right, (((1,), (1,)), ((), ())), preferred_element_type=F32)


def dot(left, right):
    return jnp.dot(left, right, preferred_element_type=F32)


def kernel(
    latent_in,
    actions_in,
    table_in,
    gain1_in,
    w_query_in,
    w_key_in,
    w_value_in,
    w_out_in,
    keys_in,
    values_in,
    gain2_in,
    policy_in_in,
    value_in_in,
    policy_out_in,
    value_out_in,
    targets_in,
    returns_in,
    latent_out,
    grads_out,
    policy_out_grad,
    misc_out,
    latent,
    actions,
    table,
    gain1,
    w_qkv,
    w_out,
    keys,
    values,
    gain2,
    heads_w,
    policy_out,
    value_out,
    targets,
    returns,
    normed,
    squares,
    tokens,
    qkv,
    attended,
    gained_t,
    pre_send,
    pre_recv,
    onehot,
    returns_col,
    dpre_send,
    dpre_recv,
    factor_send,
    factor_recv,
    misc_send,
    misc_recv,
    grad_f32,
    grad_send,
    grad_recv,
    block_f32,
    block_send,
    block_recv,
    block_mid,
    block_recv_z,
    misc_x,
    misc_z,
    load_sem,
    send_sem,
    recv_sem,
):
    wide, narrow = lax.axis_index("wide"), lax.axis_index("narrow")
    x, z = wide // Z, lax.rem(wide, Z)
    y, c = narrow // 2, lax.rem(narrow, 2)
    _, scenes, branch, width = normed.shape
    total_rows = scenes * branch * X * Z
    full_width = width * NARROW

    def device(dx=0, dy=0, dz=0, dc=0):
        return (
            lax.rem(x + dx, X) * Z + lax.rem(z + dz, Z),
            lax.rem(y + dy, Y) * 2 + lax.rem(c + dc, 2),
        )

    def span(index, size):
        return pl.ds(pl.multiple_of(index * size, size), size)

    plane = [(dx, dy, dc) for dx in (2, 1, 3, 0) for dy in (2, 1, 3, 0) for dc in (1, 0)]
    plane = [o for o in plane if o != (0, 0, 0)]
    line = [(dy, dc) for dx, dy, dc in plane if dx == 0]
    z_steps = (4, 3, 5, 2, 6, 1, 7)
    x_steps = (2, 1, 3)
    y_steps = (2, 1, 3)
    barrier = pltpu.get_barrier_semaphore()
    partners = [device(dx, dy, 0, dc) for dx, dy, dc in plane] + [device(dz=d) for d in z_steps]
    for partner in partners:
        pl.semaphore_signal(barrier, inc=1, device_id=partner, device_id_type=MESH)

    places = [narrow, y * 2 + 1 - c]
    places += [lax.rem(y - d + Y, Y) * 2 + c for d in y_steps]
    places += [lax.rem(y - d + Y, Y) * 2 + 1 - c for d in y_steps]

    loads = {}

    def load(name, target, *pieces):
        sem = load_sem.at[len(loads)]
        for source, part in pieces:
            pltpu.make_async_copy(source, part, sem).start()
        loads[name] = pltpu.make_async_copy(target, target, sem)

    def ready(*names):
        for name in names:
            loads[name].wait()
            loads[name] = None

    load("actions", actions, (actions_in, actions))
    load("table", table, (table_in, table))
    load("latent", latent, (latent_in, latent))
    load("gain1", gain1, (gain1_in, gain1))
    weights = (w_query_in, w_key_in, w_value_in)
    load(
        "w_qkv",
        w_qkv,
        *[
            (weights[i].at[span(place, width)], w_qkv.at[i, pl.ds(p * width, width)])
            for p, place in enumerate(places)
            for i in range(3)
        ],
    )
    load("keys", keys, (keys_in, keys))
    load("values", values, (values_in, values))
    depth = w_qkv.shape[2]
    load(
        "w_out",
        w_out,
        *[
            (w_out_in.at[span(place, depth)], w_out.at[pl.ds(p * depth, depth)])
            for p, place in enumerate(places)
        ],
    )
    load("gain2", gain2, (gain2_in, gain2))
    load("heads_w", heads_w, (policy_in_in, heads_w.at[0]), (value_in_in, heads_w.at[1]))
    load("policy_out", policy_out, (policy_out_in, policy_out))
    load("value_out", value_out, (value_out_in, value_out))
    load("targets", targets, (targets_in, targets))
    load("returns", returns, (returns_in, returns))

    started, pending, groups, outgoing = [], {}, {}, {}
    counts = [0]

    def group_sem(name):
        if name not in groups:
            groups[name] = (counts[0], [])
            counts[0] += 1
        return recv_sem.at[groups[name][0]]

    def send(source, target, partner, out, into=None):
        if out not in outgoing:
            outgoing[out] = len(outgoing)
        if into is None:
            arrival = recv_sem.at[counts[0]]
            counts[0] += 1
        else:
            arrival = group_sem(into)
        copy = pltpu.make_async_remote_copy(
            src_ref=source,
            dst_ref=target,
            send_sem=send_sem.at[outgoing[out]],
            recv_sem=arrival,
            device_id=partner,
            device_id_type=MESH,
        )
        copy.start()
        started.append(copy)
        if into is None:
            pending[id(copy)] = copy
        else:
            groups[into][1].append(copy)
        return copy

    def arrive(*copies):
        for copy in copies:
            copy.wait_recv()
            del pending[id(copy)]

    def collect(name, whole):
        pltpu.make_async_copy(whole, whole, recv_sem.at[groups[name][0]]).wait()
        groups[name][1].clear()

    def finish(whole=None):
        ready(*[name for name in loads if loads[name] is not None])
        arrive(*list(pending.values()))
        if whole is None:
            for copies in groups.values():
                for copy in copies[1]:
                    copy.wait_recv()
            for copy in started:
                copy.wait_send()
        else:
            for name, i in outgoing.items():
                pltpu.make_async_copy(whole[name], whole[name], send_sem.at[i]).wait()

    ready("actions", "table", "latent", "gain1")
    action_count = table.shape[0]
    action_ids = lax.broadcasted_iota(jnp.int32, (action_count, branch), 0)
    for s in range(scenes):
        chosen = (actions[s : s + 1, :] == action_ids).astype(F32).T.astype(BF16)
        token = latent[s].astype(F32) + dot(chosen, table[...])
        tokens[s] = token
        normed[0, s] = (token * gain1[...]).astype(BF16)
        square = token * token
        square = sum(square[:, i : i + 128] for i in range(0, width, 128))
        squares[0, s : s + 1, :] = jnp.sum(square.T, axis=0, keepdims=True)

    pl.semaphore_wait(barrier, len(partners))

    def gather_start(buffer, s, out):
        near = send(buffer.at[0, s], buffer.at[1, s], device(dc=1), out)
        far = [
            send(buffer.at[0, s], buffer.at[2 + i, s], device(dy=d), out)
            for i, d in enumerate(y_steps)
        ]
        return near, far

    def gather_pass(buffer, s, far, out):
        passed = []
        for i, copy in enumerate(far):
            arrive(copy)
            passed.append(send(buffer.at[2 + i, s], buffer.at[5 + i, s], device(dc=1), out))
        return passed

    def gathered(buffer, s, low, high):
        return jnp.concatenate([buffer[p, s] for p in range(low, high)], axis=1)

    gathers = [gather_start(normed, 0, "normed")]
    for dy, dc in line:
        send(squares.at[0], squares.at[2 * dy + dc], device(dy=dy, dc=dc), "squares", "squares")
    gathers.append(gather_start(normed, 1, "normed"))

    ready("targets", "returns")
    for s in range(scenes):
        onehot[s] = (targets[s : s + 1, :] == action_ids).astype(F32).T
        returns_col[s] = jnp.broadcast_to(returns[s : s + 1, :], (128, branch)).T

    scaling = HD ** (-0.5)
    heads_local = depth // HD
    attended_copies = []

    def project(s, low, high):
        rows = gathered(normed, s, low, high)
        for i in range(3):
            product = dot(rows, w_qkv[i, low * width : high * width, :])
            if low == 0:
                qkv[s, i] = product
            else:
                qkv[s, i] += product

    ready("w_qkv")
    for s in range(scenes):
        arrive(gathers[s][0])
        project(s, 0, 2)
    for s in range(scenes):
        passed = gather_pass(normed, s, gathers[s][1], "normed")
        project(s, 2, 5)
        arrive(*passed)
        project(s, 5, 8)
        if s == 0:
            collect("squares", squares.at[pl.ds(1, NARROW - 1)])
            ready("keys", "values")
        total = jnp.sum(squares[:, s : s + 1, :], axis=0)
        inverse = lax.rsqrt(total / full_width + EPSILON)
        inverse = jnp.broadcast_to(inverse, (128, branch)).T
        for h in range(heads_local):
            cols = slice(h * HD, (h + 1) * HD)
            query, key_new, value_new = (
                (qkv[s, i, :, cols] * inverse).astype(BF16) for i in range(3)
            )
            scores = nt_dot(query, keys[s, :, cols]) * scaling
            own_score = (
                jnp.sum(query.astype(F32) * key_new.astype(F32), axis=1, keepdims=True) * scaling
            )
            highest = jnp.maximum(jnp.max(scores, axis=1, keepdims=True), own_score)
            expd = jnp.exp(scores - highest)
            own_exp = jnp.exp(own_score - highest)
            share = 1.0 / (jnp.sum(expd, axis=1, keepdims=True) + own_exp)
            probs = (expd * share).astype(BF16)
            own_prob = (own_exp * share).astype(BF16).astype(F32)
            mixed = dot(probs, values[s, :, cols]) + own_prob * value_new.astype(F32)
            attended[0, s, :, cols] = mixed.astype(BF16)
        attended_copies.append(gather_start(attended, s, "attended"))

    ready("w_out", "gain2", "heads_w")
    heads_width = heads_w.shape[2]
    both = 2 * heads_width
    share_rows = branch // NARROW
    my_rows = span(narrow, share_rows)
    for s in range(scenes):
        near, far = attended_copies[s]

        def update(low, high):
            return dot(gathered(attended, s, low, high), w_out[low * depth : high * depth, :])

        arrive(near)
        tokens[s] += update(0, 2)
        passed = gather_pass(attended, s, far, "attended")
        tokens[s] += update(2, 5)
        arrive(*passed)
        state = tokens[s] + update(5, 8)
        gained = state * gain2[...]
        gained_b = gained.astype(BF16)
        for i in range(2):
            pre_send[s, :, i * heads_width : (i + 1) * heads_width] = dot(
                gained_b, heads_w[i]
            ).astype(BF16)
        square = jnp.sum(state * state, axis=1, keepdims=True)
        high = square.astype(BF16).astype(F32)
        lane = lax.broadcasted_iota(jnp.int32, (branch, 128), 1)
        pre_send[s, :, both:] = jnp.where(lane < 64, high, square - high).astype(BF16)
        for dy, dc in line:
            partner = device(dy=dy, dc=dc)
            send(
                pre_send.at[s, span(partner[1], share_rows)],
                pre_recv.at[s, 2 * dy + dc],
                partner,
                "pre",
                ("pre", s),
            )
        pre_recv[s, 0] = pre_send[s, my_rows, :]
        latent_out[s] = state.astype(BF16)
        gained_t[0, s] = gained.T.astype(BF16)
        for d in x_steps:
            send(gained_t.at[0, s], gained_t.at[d, s], device(dx=d), "gained", "gained")

    ready("policy_out", "value_out")
    for s in range(scenes):
        collect(("pre", s), pre_recv.at[s, pl.ds(1, NARROW - 1)])

    def summed(low, high):
        return jnp.concatenate(
            [
                sum(pre_recv[s, i, :, low:high].astype(F32) for i in range(NARROW))
                for s in range(scenes)
            ],
            axis=0,
        )

    square = summed(both, both + 128)
    square = square[:, 0:1] + square[:, 64:65]
    inverse = lax.rsqrt(square / full_width + EPSILON)

    def hidden_layer(low):
        pre = summed(low, low + heads_width) * inverse
        sigma = 1.0 / (1.0 + jnp.exp(-pre))
        slope = sigma * (1.0 + pre * (1.0 - sigma)) * inverse
        return (pre * sigma).astype(BF16), slope

    half = heads_width // X

    def share_dpre(i, dpre):
        for j in range(X):
            for s in range(scenes):
                dpre_send[i, j, s] = dpre[
                    s * share_rows : (s + 1) * share_rows, j * half : (j + 1) * half
                ]
        own = pltpu.make_async_copy(
            dpre_send.at[i, x], dpre_recv.at[i, 0, :, my_rows, :], group_sem(("dpre", i))
        )
        own.start()
        for dx, dy, dc in plane:
            send(
                dpre_send.at[i, lax.rem(x + dx, X)],
                dpre_recv.at[i, dx, :, my_rows, :],
                device(dx=dx, dy=dy, dc=dc),
                "dpre_y" if dx == 0 else "dpre_x",
                ("dpre", i),
            )

    factor = total_rows ** (-0.5)
    hidden, slope = hidden_layer(heads_width)
    value_hidden = hidden.astype(F32)
    value_row = value_out[...].astype(F32)
    value_row = jnp.concatenate([value_row[i : i + 1] for i in range(Y)], axis=1)
    value = jnp.sum(value_hidden * value_row, axis=1, keepdims=True)
    wanted = jnp.concatenate([returns_col[s, my_rows, :] for s in range(scenes)], axis=0)
    errors = value - wanted[:, 0:1]
    dvalue = (errors * factor).astype(BF16).astype(F32)
    share_dpre(0, (dvalue * value_row * slope).astype(BF16))

    policy_hidden, slope = hidden_layer(0)
    logits = dot(policy_hidden, policy_out[...])
    top = jnp.max(logits, axis=1, keepdims=True)
    log_total = top + jnp.log(jnp.sum(jnp.exp(logits - top), axis=1, keepdims=True))
    target = jnp.concatenate([onehot[s, my_rows, :] for s in range(scenes)], axis=0)
    dlogits = ((jnp.exp(logits - log_total) - target) * factor).astype(BF16)
    share_dpre(1, (nt_dot(dlogits, policy_out[...]) * slope).astype(BF16))

    block = heads_width // Y
    lanes = lax.broadcasted_iota(jnp.int32, (1, 128), 1)
    picked = jnp.sum(logits * target, axis=1, keepdims=True)
    sum_policy = jnp.sum(log_total - picked, axis=0, keepdims=True)
    sum_value = 0.5 * jnp.sum(errors * errors, axis=0, keepdims=True)
    loss_row = jnp.where(lanes == 0, sum_policy, jnp.where(lanes == 1, sum_value, 0.0))
    value_grad = jnp.sum(dvalue * value_hidden, axis=0, keepdims=True)
    for i in range(Y):
        for j in range(2):
            factor_send[2 * i + j, :, :block] = policy_hidden[:, i * block : (i + 1) * block]
            factor_send[2 * i + j, :, block:] = dlogits[:, j * 128 : (j + 1) * 128]
        misc_send[i] = jnp.concatenate(
            [value_grad[:, i * block : (i + 1) * block], loss_row, jnp.zeros((6, 128), F32)], axis=0
        )
    factor_recv[0] = factor_send[narrow]
    misc_recv[0] = misc_send[y]
    for dy, dc in line:
        partner, i = device(dy=dy, dc=dc), 2 * dy + dc
        send(factor_send.at[partner[1]], factor_recv.at[i], partner, "factor", "factor")
        send(misc_send.at[lax.rem(y + dy, Y)], misc_recv.at[i], partner, "misc", "misc")

    collect("gained", gained_t.at[pl.ds(1, X - 1)])
    state_t = jnp.concatenate(
        [gained_t[i, s] for i in range(X) for s in range(scenes)], axis=1
    )
    grad_rows = width // Z
    my_grad = span(z, grad_rows)
    for i in range(2):
        collect(("dpre", i), dpre_recv.at[i])
        grad = dot(
            state_t,
            jnp.concatenate([dpre_recv[i, j, s] for j in range(X) for s in range(scenes)], axis=0),
        )
        grad_f32[i] = grad
        grad_send[i] = grad.astype(BF16)
        for d in z_steps:
            rows = span(lax.rem(z + d, Z), grad_rows)
            send(
                grad_send.at[i, rows], grad_recv.at[i, d - 1], device(dz=d), "grad", ("grad", i)
            )

    collect("factor", factor_recv.at[pl.ds(1, NARROW - 1)])
    collect("misc", misc_recv.at[pl.ds(1, NARROW - 1)])
    left = jnp.concatenate([factor_recv[i, :, :block] for i in range(NARROW)], axis=0)
    right = jnp.concatenate([factor_recv[i, :, block:] for i in range(NARROW)], axis=0)
    part = dot(left.astype(F32).T.astype(BF16), right)
    block_f32[...] = part
    block_send[...] = part.astype(BF16)
    misc_x[0] = sum(misc_recv[i] for i in range(NARROW))
    block_rows = block // X
    for d in x_steps:
        rows = span(lax.rem(x + d, X), block_rows)
        send(block_send.at[rows], block_recv.at[d - 1], device(dx=d), "block", "block")
        send(misc_x.at[0], misc_x.at[d], device(dx=d), "misc_x", "misc_x")

    def spread(i, rows, out, into=None, **step):
        place = grads_out.at[1 - i, rows, span(x, half)]
        return send(place, place, device(**step), out, into)

    def spread_x(i, rows):
        for d in x_steps:
            spread(i, rows, "x", ("x", i, d), dx=d)

    along_z = []
    for i in range(2):
        collect(("grad", i), grad_recv.at[i])
        reduced = grad_f32[i, my_grad, :] + sum(grad_recv[i, j].astype(F32) for j in range(Z - 1))
        grads_out[1 - i, my_grad, span(x, half)] = reduced.astype(BF16)
        along_z.append({d: spread(i, my_grad, "z", dz=d) for d in z_steps})
        spread_x(i, my_grad)
        if i == 0:
            collect("block", block_recv)
            collect("misc_x", misc_x.at[pl.ds(1, X - 1)])
            block_sum = block_f32[span(x, block_rows), :]
            block_sum = block_sum + sum(block_recv[j].astype(F32) for j in range(X - 1))
            block_mid[...] = block_sum.astype(BF16)
            misc_z[0] = sum(misc_x[j] for j in range(X))
            for d in z_steps:
                send(block_mid, block_recv_z.at[d - 1], device(dz=d), "block_z", "block_z")
                send(misc_z.at[0], misc_z.at[d], device(dz=d), "misc_z", "misc_z")

    def forward(i, *steps):
        for d in steps:
            arrive(along_z[i][d])
            spread_x(i, span(lax.rem(z - d + Z, Z), grad_rows))

    forward(0, 1, 7, 2, 6)
    collect("block_z", block_recv_z)
    collect("misc_z", misc_z.at[pl.ds(1, Z - 1)])
    reduced = block_sum + sum(block_recv_z[i].astype(F32) for i in range(Z - 1))
    block_cols = span(c, 128)
    place = policy_out_grad.at[span(y * X + x, block_rows), block_cols]
    place[...] = reduced.astype(BF16)
    block_copies = [send(place, place, device(dx=d), "block_x") for d in x_steps]
    misc_out[y] = sum(misc_z[i] for i in range(Z))
    for d in y_steps:
        send(misc_out.at[y], misc_out.at[y], device(dy=d), "misc_y")
    forward(0, 3, 5, 4)
    arrive(*block_copies)
    place = policy_out_grad.at[span(y, block), block_cols]
    for dy, dc in line:
        send(place, place, device(dy=dy, dc=dc), "block_y")
    forward(1, 1, 7, 2, 6, 3, 5, 4)
    for i in range(2):
        for d in x_steps:
            collect(("x", i, d), grads_out.at[1 - i, :, span(lax.rem(x - d + X, X), half)])
    finish(
        {
            "normed": normed.at[pl.ds(0, 7)],
            "squares": squares.at[pl.ds(0, 7)],
            "attended": attended.at[pl.ds(0, 7)],
            "pre": pre_recv.at[:, pl.ds(0, 7)],
            "gained": gained_t.at[pl.ds(0, 3)],
            "dpre_x": dpre_recv.at[:, pl.ds(0, 3)],
            "dpre_y": dpre_recv.at[:, 0, :, pl.ds(0, 7 * share_rows), :],
            "factor": factor_recv.at[pl.ds(0, 7)],
            "misc": misc_recv.at[pl.ds(0, 7)],
            "grad": grad_recv,
            "block": block_recv,
            "misc_x": misc_x.at[pl.ds(0, 3)],
            "z": grads_out.at[:, pl.ds(0, 112), :],
            "x": grads_out.at[:, pl.ds(0, 384), :],
            "block_z": block_recv_z,
            "misc_z": misc_z.at[pl.ds(0, 7)],
            "block_x": policy_out_grad.at[pl.ds(0, 48)],
            "misc_y": misc_out.at[pl.ds(0, 3)],
            "block_y": policy_out_grad.at[pl.ds(0, 448)],
        }
    )


def deliver(
    total_rows,
    latent,
    grads,
    policy_out_grad,
    misc,
    latent_to,
    policy_in_to,
    value_in_to,
    policy_out_to,
    losses_to,
    value_out_to,
    losses,
    value_out_grad,
    sem,
):
    copies = [
        pltpu.make_async_copy(source, target, sem.at[i])
        for i, (source, target) in enumerate(
            (
                (grads.at[0], policy_in_to),
                (grads.at[1], value_in_to),
                (latent, latent_to),
                (policy_out_grad, policy_out_to),
                (losses, losses_to),
                (value_out_grad, value_out_to),
            )
        )
    ]
    for copy in copies[:4]:
        copy.start()
    losses[...] = misc[0, 1:2, :2] * (1.0 / total_rows)
    value_out_grad[...] = jnp.concatenate(
        [misc[i, 0:1, :] for i in range(misc.shape[0])], axis=0
    ).astype(BF16)
    for copy in copies[4:]:
        copy.start()
    for copy in copies:
        copy.wait()


def per_device(
    latent,
    actions,
    action_table,
    norm1_gain,
    w_query,
    w_key,
    w_value,
    w_out,
    key_cache,
    value_cache,
    norm2_gain,
    policy_in,
    value_in,
    policy_out,
    value_out,
    targets,
    returns,
):
    rows, width = latent.shape
    scenes = key_cache.shape[0]
    branch = rows // scenes
    heads_width = policy_in.shape[1]
    features = w_query.shape[1]
    share = branch // NARROW
    block = heads_width // Y
    half = heads_width // X
    total_rows = rows * X * Z
    vmem = pltpu.VMEM
    operands = (
        latent.reshape(scenes, branch, width),
        actions.reshape(scenes, branch),
        action_table,
        norm1_gain.reshape(1, width),
        w_query,
        w_key,
        w_value,
        w_out,
        key_cache,
        value_cache,
        norm2_gain.reshape(1, width),
        policy_in,
        value_in,
        policy_out,
        value_out.reshape(Y, 128),
        targets.reshape(scenes, branch),
        returns.reshape(scenes, branch),
    )
    operands = [pltpu.with_memory_space_constraint(operand, pltpu.HBM) for operand in operands]
    scratch = [
        vmem((scenes, branch, width), BF16),
        vmem((scenes, branch), jnp.int32),
        vmem(action_table.shape, BF16),
        vmem((1, width), F32),
        vmem((3,) + w_query.shape, BF16),
        vmem(w_out.shape, BF16),
        vmem(key_cache.shape, BF16),
        vmem(value_cache.shape, BF16),
        vmem((1, width), F32),
        vmem((2,) + policy_in.shape, BF16),
        vmem(policy_out.shape, BF16),
        vmem((Y, 128), BF16),
        vmem((scenes, branch), jnp.int32),
        vmem((scenes, branch), F32),
        vmem((NARROW, scenes, branch, width), BF16),
        vmem((NARROW, 8, branch), F32),
        vmem((scenes, branch, width), F32),
        vmem((scenes, 3, branch, features), F32),
        vmem((NARROW, scenes, branch, features), BF16),
        vmem((X, scenes, width, branch), BF16),
        vmem((scenes, branch, 2 * heads_width + 128), BF16),
        vmem((scenes, NARROW, share, 2 * heads_width + 128), BF16),
        vmem((scenes, branch, policy_out.shape[1]), F32),
        vmem((scenes, branch, 128), F32),
        vmem((2, X, scenes, share, half), BF16),
        vmem((2, X, scenes, branch, half), BF16),
        vmem((NARROW, scenes * share, block + 128), BF16),
        vmem((NARROW, scenes * share, block + 128), BF16),
        vmem((Y, 8, 128), F32),
        vmem((NARROW, 8, 128), F32),
        vmem((2, width, half), F32),
        vmem((2, width, half), BF16),
        vmem((2, Z - 1, width // Z, half), BF16),
        vmem((block, 128), F32),
        vmem((block, 128), BF16),
        vmem((X - 1, block // X, 128), BF16),
        vmem((block // X, 128), BF16),
        vmem((Z - 1, block // X, 128), BF16),
        vmem((X, 8, 128), F32),
        vmem((Z, 8, 128), F32),
        pltpu.SemaphoreType.DMA((LOADS,)),
        pltpu.SemaphoreType.DMA((SENDS,)),
        pltpu.SemaphoreType.DMA((ARRIVALS,)),
    ]
    results = pl.pallas_call(
        kernel,
        name="imagine",
        out_shape=(
            vmem((scenes, branch, width), BF16),
            vmem((2, width, heads_width), BF16),
            vmem(policy_out.shape, BF16),
            vmem((Y, 8, 128), F32),
        ),
        in_specs=[pl.BlockSpec(memory_space=pltpu.HBM)] * len(operands),
        out_specs=[pl.BlockSpec(memory_space=pltpu.VMEM)] * 4,
        scratch_shapes=scratch,
        compiler_params=pltpu.CompilerParams(
            collective_id=0, has_side_effects=True, vmem_limit_bytes=40 * 2**20
        ),
    )(*operands)
    new_latent, policy_in_grad, value_in_grad, policy_out_grad, losses, value_out_grad = pl.pallas_call(
        functools.partial(deliver, total_rows),
        name="deliver",
        out_shape=(
            jax.ShapeDtypeStruct((scenes, branch, width), BF16),
            jax.ShapeDtypeStruct(policy_in.shape, BF16),
            jax.ShapeDtypeStruct(value_in.shape, BF16),
            jax.ShapeDtypeStruct(policy_out.shape, BF16),
            jax.ShapeDtypeStruct((1, 2), F32),
            jax.ShapeDtypeStruct((Y, 128), BF16),
        ),
        in_specs=[pl.BlockSpec(memory_space=pltpu.VMEM)] * 4,
        out_specs=[pl.BlockSpec(memory_space=pltpu.HBM)] * 6,
        scratch_shapes=[
            vmem((1, 2), F32),
            vmem((Y, 128), BF16),
            pltpu.SemaphoreType.DMA((6,)),
        ],
        compiler_params=pltpu.CompilerParams(vmem_limit_bytes=8 * 2**20),
    )(*[pltpu.with_memory_space_constraint(result, pltpu.VMEM) for result in results])
    return (
        new_latent.reshape(rows, width),
        losses.reshape(2),
        policy_in_grad,
        value_in_grad,
        policy_out_grad,
        value_out_grad.reshape(heads_width),
    )


def solution(mesh):
    placed = (
        P("wide", "narrow"),
        P("wide"),
        P(None, "narrow"),
        P("narrow"),
        P(None, "narrow"),
        P(None, "narrow"),
        P(None, "narrow"),
        P(None, "narrow"),
        P("wide", None, "narrow"),
        P("wide", None, "narrow"),
        P("narrow"),
        P("narrow", None),
        P("narrow", None),
        P(),
        P(),
        P("wide"),
        P("wide"),
    )
    return jax.shard_map(
        per_device,
        mesh=mesh,
        in_specs=placed,
        out_specs=(P("wide", "narrow"), P(), P("narrow", None), P("narrow", None), P(), P()),
        check_vma=False,
    )
```

time: 79.4 us -> 72.6 us (0.914)
  Pallas kernels: 78.7 us -> 71.9 us
    pallas_call x1, Pallas kernels: 77.5 us -> 70.7 us  [per_device(): pl.pallas_call(kernel, name='imagine', out_shape=(vmem((scenes, branch, w...]
where the time goes in v3:
time: 72.6 us; the launch traced here: 72.5 us
  Pallas kernels  71.9 us (99%)
    pallas_call x1, Pallas kernels, per_device(): pl.pallas_call(kernel, name='imagine', out_shape=(vmem((scenes, branch, w...  70.7 us

profile of v3, /device:TPU:1, one launch (start us, length us, event | category | flops | bytes accessed | tf_op | source)
XLA Modules:
  0.0 72.5 jit_solution(17602933293044535918)
XLA Ops:
  0.6 70.7 %imagine.1 = (bf16[2,128,512]{2,1,0:T(8,128)(2,1)S(1)}, bf16[2,512,512]{2,1,0:T(8,128)(2,1)S(1)}, bf16[512,256]{1,0:T(8,128)(2,1)S(1)}, f32[4,8,128]{2,1,0:T(8,128)S(1)}) custom-call(bf16[2,128,512]{2,1,0:T(8,128)(2,1)} %bitcast.10, s32[2,128]{1,0:T(2,128)} %bitcast.13, bf16[256,512]{1,0:T(8,128)(2,1)} %table_in.1, f32[1,512]{1,0:T(1,128)} %bitcast.11, ...), custom_call_target="tpu_custom_call" | custom-call | tf_op jit(solution)/shard_map/imagine/pallas_call | solution.py:684
  71.3 1.2 %deliver.1 = (bf16[2,128,512]{2,1,0:T(8,128)(2,1)}, bf16[512,512]{1,0:T(8,128)(2,1)}, bf16[512,512]{1,0:T(8,128)(2,1)}, bf16[512,256]{1,0:T(8,128)(2,1)}, f32[1,2]{1,0:T(1,128)}, /*index=5*/bf16[4,128]{1,0:T(4,128)(2,1)}) custom-call(bf16[2,128,512]{2,1,0:T(8,128)(2,1)S(1)} %get-tuple-element.16.latent, bf16[2,512,512]{2,1,0:T(8,128)(2,1)S(1)} %get-tuple-element.17.grads, ...), custom_call_target="tpu_custom_call" | custom-call | tf_op jit(solution)/shard_map/deliver/pallas_call | solution.py:700

commit v4 on v3

--- a/solution.py
+++ b/solution.py
@@ -13,7 +13,7 @@
 NARROW = 2 * Y
 MESH = pl.DeviceIdType.MESH
 F32, BF16 = jnp.float32, jnp.bfloat16
-LOADS, SENDS, ARRIVALS = 14, 19, 75
+LOADS, SENDS, ARRIVALS = 14, 24, 81
 
 
 def nt_dot(left, right):
@@ -111,7 +111,7 @@
     line = [(dy, dc) for dx, dy, dc in plane if dx == 0]
     z_steps = (4, 3, 5, 2, 6, 1, 7)
     x_steps = (2, 1, 3)
-    y_steps = (2, 1, 3)
+    y_steps = (1, 3, 2)
     barrier = pltpu.get_barrier_semaphore()
     partners = [device(dx, dy, 0, dc) for dx, dy, dc in plane] + [device(dz=d) for d in z_steps]
     for partner in partners:
@@ -132,7 +132,6 @@
     def ready(*names):
         for name in names:
             loads[name].wait()
-            loads[name] = None
 
     load("actions", actions, (actions_in, actions))
     load("table", table, (table_in, table))
@@ -166,14 +165,14 @@
     load("targets", targets, (targets_in, targets))
     load("returns", returns, (returns_in, returns))
 
-    started, pending, groups, outgoing = [], {}, {}, {}
+    groups, outgoing = {}, {}
     counts = [0]
 
     def group_sem(name):
         if name not in groups:
-            groups[name] = (counts[0], [])
+            groups[name] = counts[0]
             counts[0] += 1
-        return recv_sem.at[groups[name][0]]
+        return recv_sem.at[groups[name]]
 
     def send(source, target, partner, out, into=None):
         if out not in outgoing:
@@ -192,34 +191,18 @@
             device_id_type=MESH,
         )
         copy.start()
-        started.append(copy)
-        if into is None:
-            pending[id(copy)] = copy
-        else:
-            groups[into][1].append(copy)
         return copy
 
     def arrive(*copies):
         for copy in copies:
             copy.wait_recv()
-            del pending[id(copy)]
 
     def collect(name, whole):
-        pltpu.make_async_copy(whole, whole, recv_sem.at[groups[name][0]]).wait()
-        groups[name][1].clear()
-
-    def finish(whole=None):
-        ready(*[name for name in loads if loads[name] is not None])
-        arrive(*list(pending.values()))
-        if whole is None:
-            for copies in groups.values():
-                for copy in copies[1]:
-                    copy.wait_recv()
-            for copy in started:
-                copy.wait_send()
-        else:
-            for name, i in outgoing.items():
-                pltpu.make_async_copy(whole[name], whole[name], send_sem.at[i]).wait()
+        pltpu.make_async_copy(whole, whole, recv_sem.at[groups[name]]).wait()
+
+    def finish(whole):
+        for name, i in outgoing.items():
+            pltpu.make_async_copy(whole[name], whole[name], send_sem.at[i]).wait()
 
     ready("actions", "table", "latent", "gain1")
     action_count = table.shape[0]
@@ -329,32 +312,36 @@
         state = tokens[s] + update(5, 8)
         gained = state * gain2[...]
         gained_b = gained.astype(BF16)
-        for i in range(2):
-            pre_send[s, :, i * heads_width : (i + 1) * heads_width] = dot(
-                gained_b, heads_w[i]
-            ).astype(BF16)
+        gained_t[0, s] = gained.T.astype(BF16)
+        for d in x_steps:
+            send(gained_t.at[0, s], gained_t.at[d, s], device(dx=d), "gained", "gained")
         square = jnp.sum(state * state, axis=1, keepdims=True)
         high = square.astype(BF16).astype(F32)
         lane = lax.broadcasted_iota(jnp.int32, (branch, 128), 1)
         pre_send[s, :, both:] = jnp.where(lane < 64, high, square - high).astype(BF16)
-        for dy, dc in line:
-            partner = device(dy=dy, dc=dc)
-            send(
-                pre_send.at[s, span(partner[1], share_rows)],
-                pre_recv.at[s, 2 * dy + dc],
-                partner,
-                "pre",
-                ("pre", s),
-            )
+        for i, cols in ((1, pl.ds(heads_width, heads_width + 128)), (0, pl.ds(0, heads_width))):
+            pre_send[s, :, i * heads_width : (i + 1) * heads_width] = dot(
+                gained_b, heads_w[i]
+            ).astype(BF16)
+            for dy, dc in line:
+                partner = device(dy=dy, dc=dc)
+                send(
+                    pre_send.at[s, span(partner[1], share_rows), cols],
+                    pre_recv.at[s, 2 * dy + dc, :, cols],
+                    partner,
+                    "pre",
+                    ("pre", s, i),
+                )
         pre_recv[s, 0] = pre_send[s, my_rows, :]
         latent_out[s] = state.astype(BF16)
-        gained_t[0, s] = gained.T.astype(BF16)
-        for d in x_steps:
-            send(gained_t.at[0, s], gained_t.at[d, s], device(dx=d), "gained", "gained")
 
     ready("policy_out", "value_out")
-    for s in range(scenes):
-        collect(("pre", s), pre_recv.at[s, pl.ds(1, NARROW - 1)])
+
+    def first_layer_sums(i, start, size):
+        for s in range(scenes):
+            collect(("pre", s, i), pre_recv.at[s, pl.ds(1, NARROW - 1), :, pl.ds(start, size)])
+
+    first_layer_sums(1, heads_width, heads_width + 128)
 
     def summed(low, high):
         return jnp.concatenate(
@@ -384,17 +371,18 @@
                     s * share_rows : (s + 1) * share_rows, j * half : (j + 1) * half
                 ]
         own = pltpu.make_async_copy(
-            dpre_send.at[i, x], dpre_recv.at[i, 0, :, my_rows, :], group_sem(("dpre", i))
+            dpre_send.at[i, x], dpre_recv.at[i, c, 0, :, y], group_sem(("dpre", i))
         )
         own.start()
         for dx, dy, dc in plane:
-            send(
-                dpre_send.at[i, lax.rem(x + dx, X)],
-                dpre_recv.at[i, dx, :, my_rows, :],
-                device(dx=dx, dy=dy, dc=dc),
-                "dpre_y" if dx == 0 else "dpre_x",
-                ("dpre", i),
-            )
+            if dc == 0:
+                send(
+                    dpre_send.at[i, lax.rem(x + dx, X)],
+                    dpre_recv.at[i, c, dx, :, y],
+                    device(dx=dx, dy=dy),
+                    "dpre_y" if dx == 0 else "dpre_x",
+                    ("dpre", i),
+                )
 
     factor = total_rows ** (-0.5)
     hidden, slope = hidden_layer(heads_width)
@@ -407,6 +395,7 @@
     dvalue = (errors * factor).astype(BF16).astype(F32)
     share_dpre(0, (dvalue * value_row * slope).astype(BF16))
 
+    first_layer_sums(0, 0, heads_width)
     policy_hidden, slope = hidden_layer(0)
     logits = dot(policy_hidden, policy_out[...])
     top = jnp.max(logits, axis=1, keepdims=True)
@@ -443,11 +432,16 @@
     grad_rows = width // Z
     my_grad = span(z, grad_rows)
     for i in range(2):
-        collect(("dpre", i), dpre_recv.at[i])
-        grad = dot(
-            state_t,
-            jnp.concatenate([dpre_recv[i, j, s] for j in range(X) for s in range(scenes)], axis=0),
-        )
+        collect(("dpre", i), dpre_recv.at[i, c])
+        arrive(send(dpre_recv.at[i, c], dpre_recv.at[i, c], device(dc=1), "dpre_c"))
+        dpre = [
+            dpre_recv[i, core, j, s, k]
+            for j in range(X)
+            for s in range(scenes)
+            for k in range(Y)
+            for core in range(2)
+        ]
+        grad = dot(state_t, jnp.concatenate(dpre, axis=0))
         grad_f32[i] = grad
         grad_send[i] = grad.astype(BF16)
         for d in z_steps:
@@ -476,15 +470,28 @@
 
     def spread_x(i, rows):
         for d in x_steps:
-            spread(i, rows, "x", ("x", i, d), dx=d)
+            spread(i, rows, ("x", i), ("x", i, d), dx=d)
+
+    first_rows = grad_rows // 4
+
+    def over_z_first(i, place):
+        if i == 0:
+            return span(place, grad_rows)
+        start = pl.multiple_of(place * grad_rows + first_rows, first_rows)
+        return pl.ds(start, grad_rows - first_rows)
+
+    my_first = pl.ds(pl.multiple_of(z * grad_rows, grad_rows), first_rows)
 
     along_z = []
     for i in range(2):
         collect(("grad", i), grad_recv.at[i])
         reduced = grad_f32[i, my_grad, :] + sum(grad_recv[i, j].astype(F32) for j in range(Z - 1))
         grads_out[1 - i, my_grad, span(x, half)] = reduced.astype(BF16)
-        along_z.append({d: spread(i, my_grad, "z", dz=d) for d in z_steps})
-        spread_x(i, my_grad)
+        along_z.append({d: spread(i, over_z_first(i, z), ("z", i), dz=d) for d in z_steps})
+        if i == 1:
+            for d in x_steps:
+                spread(i, my_first, "first_x", "first_x", dx=d)
+        spread_x(i, over_z_first(i, z))
         if i == 0:
             collect("block", block_recv)
             collect("misc_x", misc_x.at[pl.ds(1, X - 1)])
@@ -499,9 +506,13 @@
     def forward(i, *steps):
         for d in steps:
             arrive(along_z[i][d])
-            spread_x(i, span(lax.rem(z - d + Z, Z), grad_rows))
+            spread_x(i, over_z_first(i, lax.rem(z - d + Z, Z)))
 
     forward(0, 1, 7, 2, 6)
+    collect("first_x", grads_out.at[0, pl.ds(0, 3 * first_rows), pl.ds(0, half)])
+    for d in z_steps:
+        rows = grads_out.at[0, my_first]
+        send(rows, rows, device(dz=d), "first_z", "first_z")
     collect("block_z", block_recv_z)
     collect("misc_z", misc_z.at[pl.ds(1, Z - 1)])
     reduced = block_sum + sum(block_recv_z[i].astype(F32) for i in range(Z - 1))
@@ -510,17 +521,17 @@
     place[...] = reduced.astype(BF16)
     block_copies = [send(place, place, device(dx=d), "block_x") for d in x_steps]
     misc_out[y] = sum(misc_z[i] for i in range(Z))
-    for d in y_steps:
-        send(misc_out.at[y], misc_out.at[y], device(dy=d), "misc_y")
+    misc_copies = [send(misc_out.at[y], misc_out.at[y], device(dy=d), "misc_y") for d in y_steps]
     forward(0, 3, 5, 4)
     arrive(*block_copies)
     place = policy_out_grad.at[span(y, block), block_cols]
-    for dy, dc in line:
-        send(place, place, device(dy=dy, dc=dc), "block_y")
+    block_copies = [send(place, place, device(dy=dy, dc=dc), "block_y") for dy, dc in line]
     forward(1, 1, 7, 2, 6, 3, 5, 4)
-    for i in range(2):
+    arrive(*misc_copies, *block_copies)
+    for i, rows in ((0, width), (1, width // 4 * 3)):
         for d in x_steps:
-            collect(("x", i, d), grads_out.at[1 - i, :, span(lax.rem(x - d + X, X), half)])
+            collect(("x", i, d), grads_out.at[1 - i, pl.ds(0, rows), span(lax.rem(x - d + X, X), half)])
+    collect("first_z", grads_out.at[0, pl.ds(0, 7 * first_rows)])
     finish(
         {
             "normed": normed.at[pl.ds(0, 7)],
@@ -528,15 +539,20 @@
             "attended": attended.at[pl.ds(0, 7)],
             "pre": pre_recv.at[:, pl.ds(0, 7)],
             "gained": gained_t.at[pl.ds(0, 3)],
-            "dpre_x": dpre_recv.at[:, pl.ds(0, 3)],
-            "dpre_y": dpre_recv.at[:, 0, :, pl.ds(0, 7 * share_rows), :],
+            "dpre_x": dpre_recv.at[:, 0, pl.ds(0, 3)],
+            "dpre_y": dpre_recv.at[:, 0, 0, :, pl.ds(0, 3)],
+            "dpre_c": dpre_recv.at[:, 0],
             "factor": factor_recv.at[pl.ds(0, 7)],
             "misc": misc_recv.at[pl.ds(0, 7)],
             "grad": grad_recv,
             "block": block_recv,
             "misc_x": misc_x.at[pl.ds(0, 3)],
-            "z": grads_out.at[:, pl.ds(0, 112), :],
-            "x": grads_out.at[:, pl.ds(0, 384), :],
+            ("z", 0): grads_out.at[0, pl.ds(0, 112)],
+            ("z", 1): grads_out.at[0, pl.ds(0, 336), pl.ds(0, 128)],
+            ("x", 0): grads_out.at[0, pl.ds(0, 384)],
+            ("x", 1): grads_out.at[0, pl.ds(0, 288)],
+            "first_x": grads_out.at[0, pl.ds(0, 48), pl.ds(0, 128)],
+            "first_z": grads_out.at[0, pl.ds(0, 112)],
             "block_z": block_recv_z,
             "misc_z": misc_z.at[pl.ds(0, 7)],
             "block_x": policy_out_grad.at[pl.ds(0, 48)],
@@ -662,7 +678,7 @@
         vmem((scenes, branch, policy_out.shape[1]), F32),
         vmem((scenes, branch, 128), F32),
         vmem((2, X, scenes, share, half), BF16),
-        vmem((2, X, scenes, branch, half), BF16),
+        vmem((2, 2, X, scenes, Y, share, half), BF16),
         vmem((NARROW, scenes * share, block + 128), BF16),
         vmem((NARROW, scenes * share, block + 128), BF16),
         vmem((Y, 8, 128), F32),

time: 72.6 us -> 72.1 us (level)
  no operation moved by 1% of the time
where the time goes in v4:
time: 72.1 us
  Pallas kernels  71.4 us (99%)
    pallas_call x1, Pallas kernels, per_device(): pl.pallas_call(kernel, name='imagine', out_shape=(vmem((scenes, branch, w...  70.2 us

profile of v4, /device:TPU:1, one launch (start us, length us, event | category | flops | bytes accessed | tf_op | source)
XLA Modules:
  0.0 72.1 jit_solution(13224108405782768277)
XLA Ops:
  0.6 70.2 %imagine.1 = (bf16[2,128,512]{2,1,0:T(8,128)(2,1)S(1)}, bf16[2,512,512]{2,1,0:T(8,128)(2,1)S(1)}, bf16[512,256]{1,0:T(8,128)(2,1)S(1)}, f32[4,8,128]{2,1,0:T(8,128)S(1)}) custom-call(bf16[2,128,512]{2,1,0:T(8,128)(2,1)} %bitcast.10, s32[2,128]{1,0:T(2,128)} %bitcast.13, bf16[256,512]{1,0:T(8,128)(2,1)} %table_in.1, f32[1,512]{1,0:T(1,128)} %bitcast.11, ...), custom_call_target="tpu_custom_call" | custom-call | tf_op jit(solution)/shard_map/imagine/pallas_call | solution.py:700
  70.9 1.2 %deliver.1 = (bf16[2,128,512]{2,1,0:T(8,128)(2,1)}, bf16[512,512]{1,0:T(8,128)(2,1)}, bf16[512,512]{1,0:T(8,128)(2,1)}, bf16[512,256]{1,0:T(8,128)(2,1)}, f32[1,2]{1,0:T(1,128)}, /*index=5*/bf16[4,128]{1,0:T(4,128)(2,1)}) custom-call(bf16[2,128,512]{2,1,0:T(8,128)(2,1)S(1)} %get-tuple-element.16.latent, bf16[2,512,512]{2,1,0:T(8,128)(2,1)S(1)} %get-tuple-element.17.grads, ...), custom_call_target="tpu_custom_call" | custom-call | tf_op jit(solution)/shard_map/deliver/pallas_call | solution.py:716
